TPU v7x, 32 devices: a whole 2x2x4 slice. The times are simulated.
32 devices in a mesh: ctx: 16 (over z, y, core), kvh: 2 (over x).
Axes of the slice: x: 2, y: 2, z: 4, core: 2. Of those that a mesh axis runs over, the one named last changes fastest.
Arguments:
- queries: bfloat16 [256, 128, 128], P(('ctx', 'kvh')), may hold values from -6 to 6
- new_keys: bfloat16 [256, 8, 128], P('ctx', 'kvh'), may hold values from -6 to 6
- new_values: bfloat16 [256, 8, 128], P('ctx', 'kvh'), may hold values from -6 to 6
- new_positions: int32 [256], P('ctx'), may hold values from 0 to 255, each once
- hist_keys: bfloat16 [48, 128, 8, 128], P('ctx', None, 'kvh'), may hold values from -6 to 6
- hist_values: bfloat16 [48, 128, 8, 128], P('ctx', None, 'kvh'), may hold values from -6 to 6
- page_slots: int32 [32], replicated, may hold values from 0 to 47, as said below
Outputs:
- attention: bfloat16 [256, 128, 128], P(('ctx', 'kvh'))
Inputs may be any that keep to these rules, and one draw needn't show every extreme that they name: `page_slots`: entry p equals 3 * d + s: history page p is held in slot s of index d of ctx. Page p belongs to index p // 2, and d is that index or the one 16 // 2 away; an index holds at most one page that belongs to that other index and at most 3 pages in all; no slot holds two pages; slots that hold no page carry data that is not part of the history.
All inputs are finite; a program needn't handle non-finite values.
Results may differ from a plain program's by a relative error of at most 0.01.
Values may be sent and summed in bfloat16 or wider, within the bound.
A program may use at most 64 MiB of HBM per device.

v0:
```python
import math

import jax
import jax.numpy as jnp
from jax import lax
from jax.sharding import PartitionSpec as P


def passed_along(block, axis, distance):
    devices = range(lax.axis_size(axis))
    route = [((i - distance) % len(devices), i) for i in devices]
    return lax.ppermute(block, axis, route)


def attend(running, kv_block, visible, grouped, scale):
    row_top, row_total, weighted = running
    scores = (
        jnp.einsum("tgqd,kgd->tgqk", grouped, kv_block[0], preferred_element_type=jnp.float32)
        * scale
    )
    masked_in = visible[:, None, None, :]
    scores = jnp.where(masked_in, scores, -1e30)
    new_top = jnp.maximum(row_top, jnp.max(scores, axis=-1))
    factor = jnp.exp(row_top - new_top)
    weights = jnp.where(masked_in, jnp.exp(scores - new_top[..., None]), 0.0)
    row_total = row_total * factor + jnp.sum(weights, axis=-1)
    rounded = weights.astype(jnp.bfloat16)
    update = jnp.einsum("tgqk,kgd->tgqd", rounded, kv_block[1], preferred_element_type=jnp.float32)
    weighted = weighted * factor[..., None] + update
    return (new_top, row_total, weighted)


def body(queries, new_keys, new_values, new_positions, hist_keys, hist_values, page_slots):
    cycle_size = lax.axis_size("ctx")
    own_index = lax.axis_index("ctx")
    local_queries = lax.all_to_all(queries, "kvh", split_axis=1, concat_axis=0, tiled=True)
    tokens_here, heads_here, width = local_queries.shape
    kv_groups = new_keys.shape[1]
    per_group = heads_here // kv_groups
    grouped = local_queries.reshape(tokens_here, kv_groups, per_group, width)
    scale = 1.0 / math.sqrt(width)
    all_positions = lax.all_gather(new_positions, "ctx", axis=0, tiled=True)
    slots_dev = hist_keys.shape[0]
    page_len = hist_keys.shape[1]
    slot_pool = jnp.stack([hist_keys, hist_values])
    fresh_kv = jnp.stack([new_keys, new_values])
    kv_block = slot_pool.reshape(2, slots_dev * page_len, kv_groups, width)
    slot_ids = jnp.arange(cycle_size * slots_dev, dtype=jnp.int32)
    live_slots = jnp.any(page_slots[None, :] == slot_ids[:, None], axis=1)

    def history_seen(source):
        live = lax.dynamic_slice_in_dim(live_slots, source * slots_dev, slots_dev)
        return jnp.repeat(live, page_len)

    history_len = kv_block.shape[1]
    running = (
        jnp.full((tokens_here, kv_groups, per_group), -1e30, jnp.float32),
        jnp.zeros((tokens_here, kv_groups, per_group), jnp.float32),
        jnp.zeros((tokens_here, kv_groups, per_group, width), jnp.float32),
    )
    carried = jnp.concatenate([kv_block, fresh_kv], axis=1)

    def visible_for(source):
        key_positions = lax.dynamic_slice_in_dim(all_positions, source * tokens_here, tokens_here)
        fresh_seen = key_positions[None, :] <= new_positions[:, None]
        seen_history = jnp.broadcast_to(history_seen(source)[None, :], (tokens_here, history_len))
        return jnp.concatenate([seen_history, fresh_seen], axis=1)

    running = attend(running, carried, visible_for(own_index), grouped, scale)

    def advance(step_index, loop_state):
        inner, moving = loop_state
        moving = passed_along(moving, "ctx", 1)
        source = (own_index - step_index) % cycle_size
        inner = attend(inner, moving, visible_for(source), grouped, scale)
        return (inner, moving)

    running, carried = lax.fori_loop(1, cycle_size, advance, (running, carried))
    row_top, row_total, weighted = running
    result = (weighted / row_total[..., None]).astype(jnp.bfloat16)
    result = result.reshape(tokens_here, heads_here, width)
    return lax.all_to_all(result, "kvh", split_axis=0, concat_axis=1, tiled=True)


def solution(mesh):
    in_specs = (
        P(("ctx", "kvh"), None, None),
        P("ctx", "kvh", None),
        P("ctx", "kvh", None),
        P("ctx"),
        P("ctx", None, "kvh", None),
        P("ctx", None, "kvh", None),
        P(),
    )
    out_specs = P(("ctx", "kvh"), None, None)
    return jax.shard_map(body, mesh=mesh, in_specs=in_specs, out_specs=out_specs, check_vma=False)
```

profile of v0, /device:TPU:0, one launch (start us, length us, event | category | flops | bytes accessed | tf_op | source)
XLA Modules:
  0.0 290.7 jit_solution(830223997603984940)
XLA Ops:
  0.0 1.9 copy.46
  1.9 4.2 %all-to-all-start = ((bf16[8,128,128]{2,0,1:T(8,128)(2,1)}), bf16[8,128,128]{2,0,1:T(8,128)(2,1)S(1)}, u32[]{:S(2)}, u32[]{:S(2)}) async-start(bf16[8,128,128]{2,0,1:T(8,128)(2,1)} %copy.46), calls=%async_computation | async-start | bytes 524288 | tf_op jit(solution)/shard_map/all_to_all | solution.py:36
  6.1 1.3 dynamic-slice
  8.9 13.0 %all-reduce = s32[256]{0:T(256)S(1)} all-reduce(s32[256]{0:T(256)S(1)} %dynamic-update-slice), channel_id=1, replica_groups=mesh['ctx'=16,'kvh'=2] {'ctx'}, use_global_device_ids=true, to_apply=%add | all-reduce | flops 256 | bytes 2048
  23.6 1.1 copy.42
  27.2 254.3 %while.21 = (s32[]{:T(128)}, f32[16,4,16]{2,0,1:T(8,128)S(1)}, f32[16,4,16]{2,0,1:T(8,128)S(1)}, f32[16,4,16,128]{3,2,0,1:T(8,128)S(1)}, bf16[2,400,4,128]{3,1,2...) while((s32[]{:T(128)}, f32[16,4,16]{2,0,1:T(8,128)S(1)}, ...), condition=%wide.region_6.7_spmd, body=%wide.region_3.6_spmd.sunk | while | flops 215310880 | bytes 12573908 | solution.py:78
  27.6 14.1 %collective-permute-done = bf16[2,400,4,128]{3,1,2,0:T(8,128)(2,1)S(1)} collective-permute-done((bf16[2,400,4,128]{3,1,2,0:T(8,128)(2,1)S(1)}, bf16[2,400,4,128]{3,1,2,0:T(8,128)(2,1)S(1)}, u32[]{:S(2)}, u32[]{:S(2)}) %collective-permute-start) | collective-permute-done | bytes 819232 | tf_op jit(solution)/shard_map/while/body/eval_jaxpr/ppermute | solution.py:12
  43.2 0.9 fusion.40
  44.6 14.1 %collective-permute-done = bf16[2,400,4,128]{3,1,2,0:T(8,128)(2,1)S(1)} collective-permute-done((bf16[2,400,4,128]{3,1,2,0:T(8,128)(2,1)S(1)}, bf16[2,400,4,128]{3,1,2,0:T(8,128)(2,1)S(1)}, u32[]{:S(2)}, u32[]{:S(2)}) %collective-permute-start) | collective-permute-done | bytes 819232 | tf_op jit(solution)/shard_map/while/body/eval_jaxpr/ppermute | solution.py:12
  60.1 0.9 fusion.40
  61.5 14.1 %collective-permute-done = bf16[2,400,4,128]{3,1,2,0:T(8,128)(2,1)S(1)} collective-permute-done((bf16[2,400,4,128]{3,1,2,0:T(8,128)(2,1)S(1)}, bf16[2,400,4,128]{3,1,2,0:T(8,128)(2,1)S(1)}, u32[]{:S(2)}, u32[]{:S(2)}) %collective-permute-start) | collective-permute-done | bytes 819232 | tf_op jit(solution)/shard_map/while/body/eval_jaxpr/ppermute | solution.py:12
  77.1 0.9 fusion.40
  78.5 14.1 %collective-permute-done = bf16[2,400,4,128]{3,1,2,0:T(8,128)(2,1)S(1)} collective-permute-done((bf16[2,400,4,128]{3,1,2,0:T(8,128)(2,1)S(1)}, bf16[2,400,4,128]{3,1,2,0:T(8,128)(2,1)S(1)}, u32[]{:S(2)}, u32[]{:S(2)}) %collective-permute-start) | collective-permute-done | bytes 819232 | tf_op jit(solution)/shard_map/while/body/eval_jaxpr/ppermute | solution.py:12
  94.1 0.9 fusion.40
  95.4 14.1 %collective-permute-done = bf16[2,400,4,128]{3,1,2,0:T(8,128)(2,1)S(1)} collective-permute-done((bf16[2,400,4,128]{3,1,2,0:T(8,128)(2,1)S(1)}, bf16[2,400,4,128]{3,1,2,0:T(8,128)(2,1)S(1)}, u32[]{:S(2)}, u32[]{:S(2)}) %collective-permute-start) | collective-permute-done | bytes 819232 | tf_op jit(solution)/shard_map/while/body/eval_jaxpr/ppermute | solution.py:12
  111.0 0.9 fusion.40
  112.4 14.1 %collective-permute-done = bf16[2,400,4,128]{3,1,2,0:T(8,128)(2,1)S(1)} collective-permute-done((bf16[2,400,4,128]{3,1,2,0:T(8,128)(2,1)S(1)}, bf16[2,400,4,128]{3,1,2,0:T(8,128)(2,1)S(1)}, u32[]{:S(2)}, u32[]{:S(2)}) %collective-permute-start) | collective-permute-done | bytes 819232 | tf_op jit(solution)/shard_map/while/body/eval_jaxpr/ppermute | solution.py:12
  128.0 0.9 fusion.40
  129.3 14.1 %collective-permute-done = bf16[2,400,4,128]{3,1,2,0:T(8,128)(2,1)S(1)} collective-permute-done((bf16[2,400,4,128]{3,1,2,0:T(8,128)(2,1)S(1)}, bf16[2,400,4,128]{3,1,2,0:T(8,128)(2,1)S(1)}, u32[]{:S(2)}, u32[]{:S(2)}) %collective-permute-start) | collective-permute-done | bytes 819232 | tf_op jit(solution)/shard_map/while/body/eval_jaxpr/ppermute | solution.py:12
  146.3 14.1 %collective-permute-done = bf16[2,400,4,128]{3,1,2,0:T(8,128)(2,1)S(1)} collective-permute-done((bf16[2,400,4,128]{3,1,2,0:T(8,128)(2,1)S(1)}, bf16[2,400,4,128]{3,1,2,0:T(8,128)(2,1)S(1)}, u32[]{:S(2)}, u32[]{:S(2)}) %collective-permute-start) | collective-permute-done | bytes 819232 | tf_op jit(solution)/shard_map/while/body/eval_jaxpr/ppermute | solution.py:12
  161.9 0.9 fusion.40
  163.2 14.1 %collective-permute-done = bf16[2,400,4,128]{3,1,2,0:T(8,128)(2,1)S(1)} collective-permute-done((bf16[2,400,4,128]{3,1,2,0:T(8,128)(2,1)S(1)}, bf16[2,400,4,128]{3,1,2,0:T(8,128)(2,1)S(1)}, u32[]{:S(2)}, u32[]{:S(2)}) %collective-permute-start) | collective-permute-done | bytes 819232 | tf_op jit(solution)/shard_map/while/body/eval_jaxpr/ppermute | solution.py:12
  180.2 14.1 %collective-permute-done = bf16[2,400,4,128]{3,1,2,0:T(8,128)(2,1)S(1)} collective-permute-done((bf16[2,400,4,128]{3,1,2,0:T(8,128)(2,1)S(1)}, bf16[2,400,4,128]{3,1,2,0:T(8,128)(2,1)S(1)}, u32[]{:S(2)}, u32[]{:S(2)}) %collective-permute-start) | collective-permute-done | bytes 819232 | tf_op jit(solution)/shard_map/while/body/eval_jaxpr/ppermute | solution.py:12
  195.8 0.9 fusion.40
  197.2 14.1 %collective-permute-done = bf16[2,400,4,128]{3,1,2,0:T(8,128)(2,1)S(1)} collective-permute-done((bf16[2,400,4,128]{3,1,2,0:T(8,128)(2,1)S(1)}, bf16[2,400,4,128]{3,1,2,0:T(8,128)(2,1)S(1)}, u32[]{:S(2)}, u32[]{:S(2)}) %collective-permute-start) | collective-permute-done | bytes 819232 | tf_op jit(solution)/shard_map/while/body/eval_jaxpr/ppermute | solution.py:12
  214.1 14.1 %collective-permute-done = bf16[2,400,4,128]{3,1,2,0:T(8,128)(2,1)S(1)} collective-permute-done((bf16[2,400,4,128]{3,1,2,0:T(8,128)(2,1)S(1)}, bf16[2,400,4,128]{3,1,2,0:T(8,128)(2,1)S(1)}, u32[]{:S(2)}, u32[]{:S(2)}) %collective-permute-start) | collective-permute-done | bytes 819232 | tf_op jit(solution)/shard_map/while/body/eval_jaxpr/ppermute | solution.py:12
  229.7 0.9 fusion.40
  231.1 14.1 %collective-permute-done = bf16[2,400,4,128]{3,1,2,0:T(8,128)(2,1)S(1)} collective-permute-done((bf16[2,400,4,128]{3,1,2,0:T(8,128)(2,1)S(1)}, bf16[2,400,4,128]{3,1,2,0:T(8,128)(2,1)S(1)}, u32[]{:S(2)}, u32[]{:S(2)}) %collective-permute-start) | collective-permute-done | bytes 819232 | tf_op jit(solution)/shard_map/while/body/eval_jaxpr/ppermute | solution.py:12
  248.0 14.1 %collective-permute-done = bf16[2,400,4,128]{3,1,2,0:T(8,128)(2,1)S(1)} collective-permute-done((bf16[2,400,4,128]{3,1,2,0:T(8,128)(2,1)S(1)}, bf16[2,400,4,128]{3,1,2,0:T(8,128)(2,1)S(1)}, u32[]{:S(2)}, u32[]{:S(2)}) %collective-permute-start) | collective-permute-done | bytes 819232 | tf_op jit(solution)/shard_map/while/body/eval_jaxpr/ppermute | solution.py:12
  263.6 0.9 fusion.40
  265.0 14.1 %collective-permute-done = bf16[2,400,4,128]{3,1,2,0:T(8,128)(2,1)S(1)} collective-permute-done((bf16[2,400,4,128]{3,1,2,0:T(8,128)(2,1)S(1)}, bf16[2,400,4,128]{3,1,2,0:T(8,128)(2,1)S(1)}, u32[]{:S(2)}, u32[]{:S(2)}) %collective-permute-start) | collective-permute-done | bytes 819232 | tf_op jit(solution)/shard_map/while/body/eval_jaxpr/ppermute | solution.py:12
  281.7 8.2 %all_to_all.33 = bf16[16,64,128]{2,1,0:T(8,128)(2,1)S(1)} all-to-all(bf16[16,64,128]{2,1,0:T(8,128)(2,1)S(1)} %bitcast.97), channel_id=1, replica_groups=mesh['ctx'=16,'kvh'=2] {'kvh'}, dimensions={0} | all-to-all | bytes 524288 | tf_op jit(solution)/shard_map/all_to_all | solution.py:82
  (231 shorter events, 38.2 us)
Async XLA Ops:
  0.0 24.6 %copy-start = (bf16[3,128,4,128]{3,2,1,0:T(4,128)(2,1)S(1)}, bf16[3,128,4,128]{3,2,1,0:T(4,128)(2,1)}, u32[]{:S(2)}) copy-start(bf16[3,128,4,128]{3,2,1,0:T(4,128)(2,1)} %param.14) | copy-start | bytes 1179652
  0.0 24.7 %copy-start.3 = (bf16[16,4,128]{2,1,0:T(4,128)(2,1)S(1)}, bf16[16,4,128]{2,1,0:T(4,128)(2,1)}, u32[]{:S(2)}) copy-start(bf16[16,4,128]{2,1,0:T(4,128)(2,1)} %param.10) | copy-start | bytes 49156
  0.0 24.7 %copy-start.2 = (bf16[16,4,128]{2,1,0:T(4,128)(2,1)S(1)}, bf16[16,4,128]{2,1,0:T(4,128)(2,1)}, u32[]{:S(2)}) copy-start(bf16[16,4,128]{2,1,0:T(4,128)(2,1)} %param.11) | copy-start | bytes 49156
  1.9 23.0 %all-to-all-start = ((bf16[8,128,128]{2,0,1:T(8,128)(2,1)}), bf16[8,128,128]{2,0,1:T(8,128)(2,1)S(1)}, u32[]{:S(2)}, u32[]{:S(2)}) async-start(bf16[8,128,128]{2,0,1:T(8,128)(2,1)} %copy.46), calls=%async_computation | async-start | bytes 524288 | tf_op jit(solution)/shard_map/all_to_all | solution.py:36
  26.4 0.8 copy-start.1
  27.2 14.5 %collective-permute-start = (bf16[2,400,4,128]{3,1,2,0:T(8,128)(2,1)S(1)}, bf16[2,400,4,128]{3,1,2,0:T(8,128)(2,1)S(1)}, u32[]{:S(2)}, u32[]{:S(2)}) collective-permute-start(bf16[2,400,4,128]{3,1,2,0:T(8,128)(2,1)S(1)} %get-tuple-element.412), channel_id=1, source_target_pairs={{30,0},{0,2},{2,4},{4,6},{6,8},{8,10},{10,12},{12,14},{14,16},{16,... | collective-permute-start | bytes 2457608 | tf_op jit(solution)/shard_map/while/body/eval_jaxpr/ppermute | solution.py:12
  44.1 14.5 %collective-permute-start = (bf16[2,400,4,128]{3,1,2,0:T(8,128)(2,1)S(1)}, bf16[2,400,4,128]{3,1,2,0:T(8,128)(2,1)S(1)}, u32[]{:S(2)}, u32[]{:S(2)}) collective-permute-start(bf16[2,400,4,128]{3,1,2,0:T(8,128)(2,1)S(1)} %get-tuple-element.412), channel_id=1, source_target_pairs={{30,0},{0,2},{2,4},{4,6},{6,8},{8,10},{10,12},{12,14},{14,16},{16,... | collective-permute-start | bytes 2457608 | tf_op jit(solution)/shard_map/while/body/eval_jaxpr/ppermute | solution.py:12
  61.1 14.5 %collective-permute-start = (bf16[2,400,4,128]{3,1,2,0:T(8,128)(2,1)S(1)}, bf16[2,400,4,128]{3,1,2,0:T(8,128)(2,1)S(1)}, u32[]{:S(2)}, u32[]{:S(2)}) collective-permute-start(bf16[2,400,4,128]{3,1,2,0:T(8,128)(2,1)S(1)} %get-tuple-element.412), channel_id=1, source_target_pairs={{30,0},{0,2},{2,4},{4,6},{6,8},{8,10},{10,12},{12,14},{14,16},{16,... | collective-permute-start | bytes 2457608 | tf_op jit(solution)/shard_map/while/body/eval_jaxpr/ppermute | solution.py:12
  78.0 14.5 %collective-permute-start = (bf16[2,400,4,128]{3,1,2,0:T(8,128)(2,1)S(1)}, bf16[2,400,4,128]{3,1,2,0:T(8,128)(2,1)S(1)}, u32[]{:S(2)}, u32[]{:S(2)}) collective-permute-start(bf16[2,400,4,128]{3,1,2,0:T(8,128)(2,1)S(1)} %get-tuple-element.412), channel_id=1, source_target_pairs={{30,0},{0,2},{2,4},{4,6},{6,8},{8,10},{10,12},{12,14},{14,16},{16,... | collective-permute-start | bytes 2457608 | tf_op jit(solution)/shard_map/while/body/eval_jaxpr/ppermute | solution.py:12
  95.0 14.5 %collective-permute-start = (bf16[2,400,4,128]{3,1,2,0:T(8,128)(2,1)S(1)}, bf16[2,400,4,128]{3,1,2,0:T(8,128)(2,1)S(1)}, u32[]{:S(2)}, u32[]{:S(2)}) collective-permute-start(bf16[2,400,4,128]{3,1,2,0:T(8,128)(2,1)S(1)} %get-tuple-element.412), channel_id=1, source_target_pairs={{30,0},{0,2},{2,4},{4,6},{6,8},{8,10},{10,12},{12,14},{14,16},{16,... | collective-permute-start | bytes 2457608 | tf_op jit(solution)/shard_map/while/body/eval_jaxpr/ppermute | solution.py:12
  112.0 14.5 %collective-permute-start = (bf16[2,400,4,128]{3,1,2,0:T(8,128)(2,1)S(1)}, bf16[2,400,4,128]{3,1,2,0:T(8,128)(2,1)S(1)}, u32[]{:S(2)}, u32[]{:S(2)}) collective-permute-start(bf16[2,400,4,128]{3,1,2,0:T(8,128)(2,1)S(1)} %get-tuple-element.412), channel_id=1, source_target_pairs={{30,0},{0,2},{2,4},{4,6},{6,8},{8,10},{10,12},{12,14},{14,16},{16,... | collective-permute-start | bytes 2457608 | tf_op jit(solution)/shard_map/while/body/eval_jaxpr/ppermute | solution.py:12
  128.9 14.5 %collective-permute-start = (bf16[2,400,4,128]{3,1,2,0:T(8,128)(2,1)S(1)}, bf16[2,400,4,128]{3,1,2,0:T(8,128)(2,1)S(1)}, u32[]{:S(2)}, u32[]{:S(2)}) collective-permute-start(bf16[2,400,4,128]{3,1,2,0:T(8,128)(2,1)S(1)} %get-tuple-element.412), channel_id=1, source_target_pairs={{30,0},{0,2},{2,4},{4,6},{6,8},{8,10},{10,12},{12,14},{14,16},{16,... | collective-permute-start | bytes 2457608 | tf_op jit(solution)/shard_map/while/body/eval_jaxpr/ppermute | solution.py:12
  145.9 14.5 %collective-permute-start = (bf16[2,400,4,128]{3,1,2,0:T(8,128)(2,1)S(1)}, bf16[2,400,4,128]{3,1,2,0:T(8,128)(2,1)S(1)}, u32[]{:S(2)}, u32[]{:S(2)}) collective-permute-start(bf16[2,400,4,128]{3,1,2,0:T(8,128)(2,1)S(1)} %get-tuple-element.412), channel_id=1, source_target_pairs={{30,0},{0,2},{2,4},{4,6},{6,8},{8,10},{10,12},{12,14},{14,16},{16,... | collective-permute-start | bytes 2457608 | tf_op jit(solution)/shard_map/while/body/eval_jaxpr/ppermute | solution.py:12
  162.8 14.5 %collective-permute-start = (bf16[2,400,4,128]{3,1,2,0:T(8,128)(2,1)S(1)}, bf16[2,400,4,128]{3,1,2,0:T(8,128)(2,1)S(1)}, u32[]{:S(2)}, u32[]{:S(2)}) collective-permute-start(bf16[2,400,4,128]{3,1,2,0:T(8,128)(2,1)S(1)} %get-tuple-element.412), channel_id=1, source_target_pairs={{30,0},{0,2},{2,4},{4,6},{6,8},{8,10},{10,12},{12,14},{14,16},{16,... | collective-permute-start | bytes 2457608 | tf_op jit(solution)/shard_map/while/body/eval_jaxpr/ppermute | solution.py:12
  179.8 14.5 %collective-permute-start = (bf16[2,400,4,128]{3,1,2,0:T(8,128)(2,1)S(1)}, bf16[2,400,4,128]{3,1,2,0:T(8,128)(2,1)S(1)}, u32[]{:S(2)}, u32[]{:S(2)}) collective-permute-start(bf16[2,400,4,128]{3,1,2,0:T(8,128)(2,1)S(1)} %get-tuple-element.412), channel_id=1, source_target_pairs={{30,0},{0,2},{2,4},{4,6},{6,8},{8,10},{10,12},{12,14},{14,16},{16,... | collective-permute-start | bytes 2457608 | tf_op jit(solution)/shard_map/while/body/eval_jaxpr/ppermute | solution.py:12
  196.7 14.5 %collective-permute-start = (bf16[2,400,4,128]{3,1,2,0:T(8,128)(2,1)S(1)}, bf16[2,400,4,128]{3,1,2,0:T(8,128)(2,1)S(1)}, u32[]{:S(2)}, u32[]{:S(2)}) collective-permute-start(bf16[2,400,4,128]{3,1,2,0:T(8,128)(2,1)S(1)} %get-tuple-element.412), channel_id=1, source_target_pairs={{30,0},{0,2},{2,4},{4,6},{6,8},{8,10},{10,12},{12,14},{14,16},{16,... | collective-permute-start | bytes 2457608 | tf_op jit(solution)/shard_map/while/body/eval_jaxpr/ppermute | solution.py:12
  213.7 14.5 %collective-permute-start = (bf16[2,400,4,128]{3,1,2,0:T(8,128)(2,1)S(1)}, bf16[2,400,4,128]{3,1,2,0:T(8,128)(2,1)S(1)}, u32[]{:S(2)}, u32[]{:S(2)}) collective-permute-start(bf16[2,400,4,128]{3,1,2,0:T(8,128)(2,1)S(1)} %get-tuple-element.412), channel_id=1, source_target_pairs={{30,0},{0,2},{2,4},{4,6},{6,8},{8,10},{10,12},{12,14},{14,16},{16,... | collective-permute-start | bytes 2457608 | tf_op jit(solution)/shard_map/while/body/eval_jaxpr/ppermute | solution.py:12
  230.6 14.5 %collective-permute-start = (bf16[2,400,4,128]{3,1,2,0:T(8,128)(2,1)S(1)}, bf16[2,400,4,128]{3,1,2,0:T(8,128)(2,1)S(1)}, u32[]{:S(2)}, u32[]{:S(2)}) collective-permute-start(bf16[2,400,4,128]{3,1,2,0:T(8,128)(2,1)S(1)} %get-tuple-element.412), channel_id=1, source_target_pairs={{30,0},{0,2},{2,4},{4,6},{6,8},{8,10},{10,12},{12,14},{14,16},{16,... | collective-permute-start | bytes 2457608 | tf_op jit(solution)/shard_map/while/body/eval_jaxpr/ppermute | solution.py:12
  247.6 14.5 %collective-permute-start = (bf16[2,400,4,128]{3,1,2,0:T(8,128)(2,1)S(1)}, bf16[2,400,4,128]{3,1,2,0:T(8,128)(2,1)S(1)}, u32[]{:S(2)}, u32[]{:S(2)}) collective-permute-start(bf16[2,400,4,128]{3,1,2,0:T(8,128)(2,1)S(1)} %get-tuple-element.412), channel_id=1, source_target_pairs={{30,0},{0,2},{2,4},{4,6},{6,8},{8,10},{10,12},{12,14},{14,16},{16,... | collective-permute-start | bytes 2457608 | tf_op jit(solution)/shard_map/while/body/eval_jaxpr/ppermute | solution.py:12
  264.6 14.5 %collective-permute-start = (bf16[2,400,4,128]{3,1,2,0:T(8,128)(2,1)S(1)}, bf16[2,400,4,128]{3,1,2,0:T(8,128)(2,1)S(1)}, u32[]{:S(2)}, u32[]{:S(2)}) collective-permute-start(bf16[2,400,4,128]{3,1,2,0:T(8,128)(2,1)S(1)} %get-tuple-element.412), channel_id=1, source_target_pairs={{30,0},{0,2},{2,4},{4,6},{6,8},{8,10},{10,12},{12,14},{14,16},{16,... | collective-permute-start | bytes 2457608 | tf_op jit(solution)/shard_map/while/body/eval_jaxpr/ppermute | solution.py:12
where the time goes:
time: 291 us
  waiting for transfers between devices  211 us (73%)
  matrix products  23.6 us (8%)
  blocking collectives  21.2 us (7%)
  other arithmetic  16.6 us (6%)
  local copies, waits for them, and re-layouts  10.6 us (4%)
  starting transfers between devices  5.08 us (2%)
    ppermute x15, waiting for transfers between devices, passed_along(): return lax.ppermute(block, axis, route)  211 us
    dot_general x16, matrix products, attend(): jnp.einsum('tgqk,kgd->tgqd', rounded, kv_block[1], preferred_element_type...  14.7 us
    reduce_sum x16, other arithmetic, attend(): row_total = row_total * factor + jnp.sum(weights, axis=-1)  13.1 us
    unnamed x1, blocking collectives  13 us
    dot_general x16, matrix products, attend(): jnp.einsum('tgqd,kgd->tgqk', grouped, kv_block[0], preferred_element_type...  8.86 us
    all_to_all x1, blocking collectives, body(): lax.all_to_all(result, 'kvh', split_axis=0, concat_axis=1, tiled=True)  8.24 us
  transfers between devices with their start and end apart: 16, of which 15 were waited for; matrix products, arithmetic and copies ran while one was open for 3% of the time, Pallas kernels for 0%

commit v1 on v0

v1 whole, which is shorter than its diff:
```python
import math

import jax
import jax.numpy as jnp
from jax import lax
from jax.experimental import pallas as pl
from jax.experimental.pallas import tpu as pltpu
from jax.sharding import PartitionSpec as P

MESH = pl.DeviceIdType.MESH
NEG = -1e30
DELAY = 2


def split_ctx(n):
    rows = max(a for a in range(1, n + 1) if n % a == 0 and a * a <= n)
    group = n // rows
    pair = 2 if group > 2 and group % 2 == 0 else 1
    return rows, group, pair


def kernel(dims, q_in, hist, new, posk, posq, bias, out,
           qbuf, kvbuf, nbuf, pkbuf, pqbuf, sbuf, pbuf, lbuf, obuf, stbuf,
           in_l, st_l, in_r, st_r, fin,
           loc_q, loc_kv, loc_n, qx_s, qx_r, qr_s, ql_s, qz_r, kv_s, kv_r, fw_s,
           n_s, n_r, pk_s, pk_r, pq_s, pq_r, or_s, ol_s, sr_s, sl_s,
           ol_r, or_r, tl_r, tr_r, ox_s, ox_r):
    A, B, B2, K, H, T, T_loc, G, HPD, SL = dims
    B1 = B // B2
    R = T * G
    c = lax.axis_index("ctx")
    k = lax.axis_index("kvh")
    z, g = c // B, c % B
    b1, b2 = g // B2, g % B2
    cc = math.log2(math.e) / math.sqrt(128)

    def remote(src, dst, ss, rs, dev):
        return pltpu.make_async_remote_copy(
            src_ref=src, dst_ref=dst, send_sem=ss, recv_sem=rs,
            device_id=dev, device_id_type=MESH)

    def heads(kk, h):
        return pl.ds(pl.multiple_of(kk * HPD + h * G, G), G)

    def toks(kk):
        return pl.ds(kk * T_loc, T_loc)

    def grp(d):
        return (g + d) % B

    def q_x(h, d):
        kk = (k + d) % K
        return remote(q_in.at[:, heads(kk, h), :], qbuf.at[h, z, toks(k)],
                      qx_s.at[h, d - 1], qx_r.at[h, d - 1], (c, kk))

    def q_x_in(h, d):
        kk = (k + K - d) % K
        dst = qbuf.at[h, z, toks(kk)]
        return remote(dst, dst, qx_s.at[h, d - 1], qx_r.at[h, d - 1], (c, kk))

    def q_loc(h):
        return pltpu.make_async_copy(q_in.at[:, heads(k, h), :], qbuf.at[h, z, toks(k)], loc_q.at[h])

    def kv_loc(h):
        return pltpu.make_async_copy(hist.at[h], kvbuf.at[h, g], loc_kv.at[h])

    def q_right(h, o):
        return remote(qbuf.at[h, o], qbuf.at[h, o], qr_s.at[h, o], qz_r.at[h, o], (c + B, k))

    def q_left(h, o):
        return remote(qbuf.at[h, o], qbuf.at[h, o], ql_s.at[h, o], qz_r.at[h, o], (c - B, k))

    def kv_far(h, d1):
        to = z * B + ((b1 + d1) % B1) * B2 + b2
        return remote(hist.at[h], kvbuf.at[h, g], kv_s.at[h, d1 - 1], kv_r.at[h, g], (to, k))

    def kv_near(h, d2):
        to = z * B + b1 * B2 + (b2 + d2) % B2
        return remote(hist.at[h], kvbuf.at[h, g], kv_s.at[h, B1 - 1 + d2 - 1], kv_r.at[h, g], (to, k))

    def kv_in(h, src):
        dst = kvbuf.at[h, src]
        return remote(dst, dst, kv_s.at[h, 0], kv_r.at[h, src], (c, k))

    def kv_pass(h, d1, d2):
        src = ((b1 + B1 - d1) % B1) * B2 + b2
        to = z * B + b1 * B2 + (b2 + d2) % B2
        return remote(kvbuf.at[h, src], kvbuf.at[h, src], fw_s.at[h, d1 - 1, d2 - 1], kv_r.at[h, src], (to, k))

    def n_out(d):
        return remote(new, nbuf.at[g], n_s.at[d - 1], n_r.at[d - 1], (z * B + grp(d), k))

    def pk_out(d):
        return remote(posk, pkbuf.at[g], pk_s.at[d - 1], pk_r.at[d - 1], (z * B + grp(d), k))

    def pq_out(d):
        return remote(posq, pqbuf.at[z], pq_s.at[d - 1], pq_r.at[d - 1], (((z + d) % A) * B + g, k))

    def n_in(d):
        src = nbuf.at[(g + B - d) % B]
        return remote(src, src, n_s.at[d - 1], n_r.at[d - 1], (c, k))

    def pk_in(d):
        src = pkbuf.at[(g + B - d) % B]
        return remote(src, src, pk_s.at[d - 1], pk_r.at[d - 1], (c, k))

    def pq_in(d):
        src = pqbuf.at[(z + A - d) % A]
        return remote(src, src, pq_s.at[d - 1], pq_r.at[d - 1], (c, k))

    def o_right(h, o):
        return (remote(obuf.at[h, o], in_l.at[h, o], or_s.at[h, o], ol_r.at[h, o], (c + B, k)),
                remote(stbuf.at[h, o], st_l.at[h, o], sr_s.at[h, o], tl_r.at[h, o], (c + B, k)))

    def o_left(h, o):
        return (remote(obuf.at[h, o], in_r.at[h, o], ol_s.at[h, o], or_r.at[h, o], (c - B, k)),
                remote(stbuf.at[h, o], st_r.at[h, o], sl_s.at[h, o], tr_r.at[h, o], (c - B, k)))

    def out_x(h, d):
        kk = (k + d) % K
        return remote(fin.at[h, toks(kk)], out.at[:, heads(k, h), :],
                      ox_s.at[h, d - 1], ox_r.at[h, d - 1], (c, kk))

    def out_x_in(h, d):
        kk = (k + K - d) % K
        dst = out.at[:, heads(kk, h), :]
        return remote(fin.at[h, toks(kk)], dst, ox_s.at[h, d - 1], ox_r.at[h, d - 1], (c, kk))

    barrier = pltpu.get_barrier_semaphore()
    for d in range(1, K):
        pl.semaphore_signal(barrier, inc=1, device_id=(c, (k + d) % K), device_id_type=MESH)
    for d in range(1, A):
        pl.semaphore_signal(barrier, inc=1, device_id=(((z + d) % A) * B + g, k), device_id_type=MESH)
    for d in range(1, B):
        pl.semaphore_signal(barrier, inc=1, device_id=(z * B + grp(d), k), device_id_type=MESH)
    pl.semaphore_wait(barrier, K - 1 + A - 1 + B - 1)

    for h in range(H):
        for d in range(1, K):
            q_x(h, d).start()
        q_loc(h).start()
        for d1 in range(1, B1):
            kv_far(h, d1).start()
        for d2 in range(1, B2):
            kv_near(h, d2).start()
        kv_loc(h).start()
        if h == 0:
            for d in range(1, B):
                n_out(d).start()
                pk_out(d).start()
            for d in range(1, A):
                pq_out(d).start()
            pltpu.make_async_copy(new, nbuf.at[g], loc_n).start()
            pkbuf[g] = posk[...]
            pqbuf[z] = posq[...]

    for h in range(H):
        q_loc(h).wait()
        for d in range(1, K):
            q_x_in(h, d).wait_recv()

        @pl.when(z < A - 1)
        def _():
            q_right(h, z).start()

        @pl.when(z > 0)
        def _():
            q_left(h, z).start()

    def q_forward(h, d):
        @pl.when(z - d >= 0)
        def _():
            q_right(h, z - d).wait_recv()

            @pl.when(z < A - 1)
            def _():
                q_right(h, z - d).start()

        @pl.when(z + d <= A - 1)
        def _():
            q_left(h, z + d).wait_recv()

            @pl.when(z > 0)
            def _():
                q_left(h, z + d).start()

    def kv_stage1(h):
        for d1 in range(1, B1):
            kv_in(h, ((b1 + B1 - d1) % B1) * B2 + b2).wait_recv()
            for d2 in range(1, B2):
                kv_pass(h, d1, d2).start()

    def kv_stage2(h):
        kv_loc(h).wait()
        for d2 in range(1, B2):
            for d1 in range(B1):
                kv_in(h, ((b1 + B1 - d1) % B1) * B2 + (b2 + B2 - d2) % B2).wait_recv()

    for d in range(1, A - 1):
        q_forward(0, d)
    kv_stage1(0)
    if A > 1:
        q_forward(0, A - 1)
    pltpu.make_async_copy(new, nbuf.at[g], loc_n).wait()
    for d in range(1, B):
        n_in(d).wait_recv()
        pk_in(d).wait_recv()
    for d in range(1, A):
        pq_in(d).wait_recv()

    low = z < A // 2
    zf = jnp.where(low, z, A - 1 - z)

    def order(j):
        far = A - 1 - zf
        f = jnp.where(j < far, A - 1 - j, jnp.where(j < A - 1, j - far, zf))
        return jnp.where(low, f, A - 1 - f)

    def attend(h, o, slot):
        q = qbuf[h, o].reshape(R, 128)
        top = jnp.full((R, 128), NEG, jnp.float32)
        for b in range(B):
            s = lax.dot_general(q, kvbuf[h, b, 0], (((1,), (1,)), ((), ())),
                                preferred_element_type=jnp.float32)
            s = s * cc + bias[8 * b:8 * b + 1, :]
            sbuf[:, b * SL:(b + 1) * SL] = s
            for i in range(SL // 128):
                top = jnp.maximum(top, s[:, i * 128:(i + 1) * 128])
        nk = nbuf[:, h, 0].reshape(B * T, 128)
        sn = lax.dot_general(q, nk, (((1,), (1,)), ((), ())), preferred_element_type=jnp.float32)
        pos_k = pkbuf[0]
        for b in range(1, B):
            pos_k = pos_k + pkbuf[b]
        pos_q = jnp.broadcast_to(pqbuf[o][:, None, :], (T, G, 128)).reshape(R, 128)
        seen = pos_k[0:1, :B * T] <= pos_q[:, :B * T]
        sn = jnp.where(seen, sn * cc, NEG)
        m = jnp.maximum(jnp.max(top, axis=-1, keepdims=True), jnp.max(sn, axis=-1, keepdims=True))
        pn = jnp.exp2(sn - m)
        nv = nbuf[:, h, 1].reshape(B * T, 128)
        acc = jnp.dot(pn.astype(jnp.bfloat16), nv, preferred_element_type=jnp.float32)
        total = jnp.zeros((R, 128), jnp.float32)
        for b in range(B):
            p = jnp.exp2(sbuf[:, b * SL:(b + 1) * SL] - m)
            for i in range(SL // 128):
                total = total + p[:, i * 128:(i + 1) * 128]
            acc = acc + jnp.dot(p.astype(jnp.bfloat16), kvbuf[h, b, 1], preferred_element_type=jnp.float32)
        denom = jnp.sum(total, axis=-1, keepdims=True) + jnp.sum(pn, axis=-1, keepdims=True)
        pbuf[slot] = acc * (1.0 / denom)
        lbuf[slot] = jnp.broadcast_to(m + jnp.log(denom) * math.log2(math.e), (R, 128))

    def merge(h, o, slot, copies, data, stats):
        for cp in copies:
            cp.wait_recv()
        x = data[h, o].astype(jnp.float32)
        for r in range(R // 128):
            rows = slice(r * 128, (r + 1) * 128)
            lx = jnp.transpose(jnp.broadcast_to(stats[h, o, 8 * r:8 * r + 1, :], (128, 128)))
            lo = lbuf[slot, rows, :]
            m = jnp.maximum(lx, lo)
            wx, wo = jnp.exp2(lx - m), jnp.exp2(lo - m)
            den = wx + wo
            pbuf[slot, rows, :] = (wx * x[rows] + wo * pbuf[slot, rows, :]) * (1.0 / den)
            lbuf[slot, rows, :] = m + jnp.log(den) * math.log2(math.e)

    def emit(h, o, slot, copies):
        obuf[h, o] = pbuf[slot].astype(jnp.bfloat16)
        for r in range(R // 128):
            stbuf[h, o, 8 * r:8 * r + 8, :] = jnp.transpose(lbuf[slot, r * 128:(r + 1) * 128, :])[0:8, :]
        for cp in copies:
            cp.start()

    steps = H * A

    def step(s, carry):
        @pl.when(s < steps)
        def _():
            h, j = s // A, s % A

            @pl.when(j == 0)
            def _():
                kv_stage2(h)

            @pl.when(h + 1 < H)
            def _():
                for d in range(1, A):
                    @pl.when(j == d - 1)
                    def _():
                        q_forward(h + 1, d)

                @pl.when(j == A - 1)
                def _():
                    kv_stage1(h + 1)

            attend(h, order(j), s % (DELAY + 1))

        @pl.when(s >= DELAY)
        def _():
            t = s - DELAY
            h, o, slot = t // A, order(t % A), t % (DELAY + 1)

            @pl.when((o >= z) & (z > 0))
            def _():
                merge(h, o, slot, o_right(h, o), in_l, st_l)

            @pl.when((o <= z) & (z < A - 1))
            def _():
                merge(h, o, slot, o_left(h, o), in_r, st_r)

            @pl.when(o > z)
            def _():
                emit(h, o, slot, o_right(h, o))

            @pl.when(o < z)
            def _():
                emit(h, o, slot, o_left(h, o))

            @pl.when(o == z)
            def _():
                fin[h] = pbuf[slot].astype(jnp.bfloat16).reshape(T, G, 128)
                for d in range(1, K):
                    out_x(h, d).start()
                out[:, heads(k, h), :] = fin[h, toks(k)]

        return carry

    lax.fori_loop(0, steps + DELAY, step, 0)

    for d in range(1, B):
        n_out(d).wait_send()
        pk_out(d).wait_send()
    for d in range(1, A):
        pq_out(d).wait_send()

    def drain(h, carry):
        for d in range(1, K):
            q_x(h, d).wait_send()
            out_x(h, d).wait_send()
            out_x_in(h, d).wait_recv()
        for d1 in range(1, B1):
            kv_far(h, d1).wait_send()
            for d2 in range(1, B2):
                kv_pass(h, d1, d2).wait_send()
        for d2 in range(1, B2):
            kv_near(h, d2).wait_send()

        def per_owner(o, inner):
            @pl.when((o <= z) & (z < A - 1))
            def _():
                q_right(h, o).wait_send()

            @pl.when((o >= z) & (z > 0))
            def _():
                q_left(h, o).wait_send()

            @pl.when(o > z)
            def _():
                for cp in o_right(h, o):
                    cp.wait_send()

            @pl.when(o < z)
            def _():
                for cp in o_left(h, o):
                    cp.wait_send()

            return inner

        lax.fori_loop(0, A, per_owner, 0)
        return carry

    lax.fori_loop(0, H, drain, 0)


def solution(mesh):
    n_ctx, K = mesh.shape["ctx"], mesh.shape["kvh"]
    A, B, B2 = split_ctx(n_ctx)
    B1 = B // B2

    def body(queries, new_keys, new_values, new_positions, hist_keys, hist_values, page_slots):
        T_loc, QH, width = queries.shape
        T, H = new_keys.shape[0], new_keys.shape[1]
        HPD = QH // K
        G = HPD // H
        slots, page = hist_keys.shape[:2]
        SL = slots * page
        R = T * G
        c = lax.axis_index("ctx")
        z, g = c // B, c % B
        hist = jnp.stack([hist_keys, hist_values]).transpose(3, 0, 1, 2, 4).reshape(H, 2, SL, width)
        new = jnp.stack([new_keys, new_values]).transpose(2, 0, 1, 3)
        lane = jnp.arange(128)
        row = jnp.where(lane // T == g, jnp.tile(new_positions, 128 // T), 0)
        posk = jnp.broadcast_to(row[None, :], (8, 128))
        posq = jnp.broadcast_to(new_positions[:, None], (T, 128))
        ids = z * B * slots + jnp.arange(B * slots, dtype=jnp.int32)
        live = jnp.any(page_slots[None, :] == ids[:, None], axis=1)
        bias = jnp.where(live, 0.0, NEG).astype(jnp.float32).reshape(B, 1, slots, 1)
        bias = jnp.broadcast_to(bias, (B, 8, slots, page)).reshape(B * 8, SL)

        bf, f32, i32 = jnp.bfloat16, jnp.float32, jnp.int32
        V = pltpu.VMEM
        D = pltpu.SemaphoreType.DMA
        kp, ap, bp = max(K - 1, 1), max(A - 1, 1), max(B - 1, 1)
        dims = (A, B, B2, K, H, T, T_loc, G, HPD, SL)
        scratch = [
            V((H, A, T, G, width), bf), V((H, B, 2, SL, width), bf), V((B, H, 2, T, width), bf),
            V((B, 8, 128), i32), V((A, T, 128), i32), V((R, B * SL), f32),
            V((DELAY + 1, R, 128), f32), V((DELAY + 1, R, 128), f32),
            V((H, A, R, 128), bf), V((H, A, R // 16, 128), f32),
            V((H, A, R, 128), bf), V((H, A, R // 16, 128), f32),
            V((H, A, R, 128), bf), V((H, A, R // 16, 128), f32),
            V((H, T, G, width), bf),
            D((H,)), D((H,)), D, D((H, kp)), D((H, kp)), D((H, A)), D((H, A)), D((H, A)),
            D((H, B)), D((H, B)), D((H, max(B1 - 1, 1), max(B2 - 1, 1))),
            D((bp,)), D((bp,)), D((bp,)), D((bp,)), D((ap,)), D((ap,)),
            D((H, A)), D((H, A)), D((H, A)), D((H, A)),
            D((H, A)), D((H, A)), D((H, A)), D((H, A)), D((H, kp)), D((H, kp)),
        ]
        any_ = pl.BlockSpec(memory_space=pl.ANY)
        vm = pl.BlockSpec(memory_space=pltpu.VMEM)
        work = A * R * (B * SL + B * T) * H
        return pl.pallas_call(
            lambda *refs: kernel(dims, *refs),
            out_shape=jax.ShapeDtypeStruct((T_loc, QH, width), bf),
            in_specs=[any_, any_, any_, vm, vm, vm],
            out_specs=vm,
            scratch_shapes=scratch,
            cost_estimate=pl.CostEstimate(flops=4 * work * width, bytes_accessed=2 * hist.size + 4 * queries.size, transcendentals=work),
            compiler_params=pltpu.CompilerParams(
                collective_id=0, has_side_effects=True, vmem_limit_bytes=40 * 1024 * 1024),
        )(queries, hist, new, posk, posq, bias)

    in_specs = (
        P(("ctx", "kvh"), None, None), P("ctx", "kvh", None), P("ctx", "kvh", None), P("ctx"),
        P("ctx", None, "kvh", None), P("ctx", None, "kvh", None), P(),
    )
    out_specs = P(("ctx", "kvh"), None, None)
    return jax.shard_map(body, mesh=mesh, in_specs=in_specs, out_specs=out_specs, check_vma=False)
```

time: 291 us -> 83.8 us (0.29)
  waiting for transfers between devices: 211 us -> 0 us
  Pallas kernels: 0 us -> 79.9 us
  matrix products: 23.6 us -> 0 us
  blocking collectives: 21.2 us -> 0 us
  other arithmetic: 16.6 us -> 1.91 us
  local copies, waits for them, and re-layouts: 10.6 us -> 1.73 us
  starting transfers between devices: 5.08 us -> 0 us
    ppermute x15 -> x0, waiting for transfers between devices: 211 us -> none  [passed_along(): return lax.ppermute(block, axis, route)]
    pallas_call x0 -> x1, Pallas kernels: none -> 79.9 us  [body(): pl.pallas_call(lambda *refs: kernel(dims, *refs), out_shape=jax.ShapeDtyp...]
    dot_general x32 -> x0, matrix products: 23.6 us -> none  [the longest x16 14.7 us: attend(): jnp.einsum('tgqk,kgd->tgqd', rounded, kv_block[1], preferred_element_type...]
    reduce_sum x16 -> x0, other arithmetic: 13.1 us -> none  [attend(): row_total = row_total * factor + jnp.sum(weights, axis=-1)]
    unnamed x1 -> x0, blocking collectives: 13 us -> none
    all_to_all x1 -> x0, blocking collectives: 8.24 us -> none  [body(): lax.all_to_all(result, 'kvh', split_axis=0, concat_axis=1, tiled=True)]
    all_to_all x1 -> x0, starting transfers between devices: 4.21 us -> none  [body(): lax.all_to_all(queries, 'kvh', split_axis=1, concat_axis=0, tiled=True)]
    unnamed x14 -> x11, local copies, waits for them, and re-layouts: 5.14 us -> 1.24 us
  transfers between devices with their start and end apart: 16 -> 0, of which waited for: 15 -> 0; matrix products, arithmetic and copies ran while one was open for 3% -> 0% of each run, Pallas kernels for 0% -> 0%
where the time goes in v1:
time: 83.8 us; the launch traced here: 83.6 us
  Pallas kernels  79.9 us (95%)
  other arithmetic  1.91 us (2%)
  local copies, waits for them, and re-layouts  1.73 us (2%)
    pallas_call x1, Pallas kernels, body(): pl.pallas_call(lambda *refs: kernel(dims, *refs), out_shape=jax.ShapeDtyp...  79.9 us
    transpose x1, other arithmetic, body(): jnp.stack([hist_keys, hist_values]).transpose(3, 0, 1, 2, 4)  1.7 us

profile of v1, /device:TPU:0, one launch (start us, length us, event | category | flops | bytes accessed | tf_op | source)
XLA Modules:
  0.0 83.6 jit_solution(14729245280406017525)
XLA Ops:
  0.0 1.7 %maximum_bitcast_fusion = bf16[4,2,3,128,128]{4,0,3,2,1:T(4,128)(2,1)S(1)} fusion(bf16[1,3,128,4,128]{4,3,2,1,0:T(4,128)(2,1)} %bitcast.14, bf16[1,3,128,4,128]{4,3,2,1,0:T(4,128)(2,1)} %bitcast.15), kind=kLoop, calls=%fused_computation | loop fusion | flops 393216 | bytes 1572864 | tf_op jit(solution)/shard_map/transpose | solution.py:388
  1.7 0.0 copy-start.1
  1.7 0.0 copy-start.2
  1.7 0.0 copy-start.3
  1.7 0.0 copy-start.4
  1.8 0.2 copy.11
  1.9 0.0 copy-start
  1.9 0.5 copy-done.1
  2.4 0.0 copy-done.2
  2.5 0.0 copy-done.3
  2.5 0.1 tile.10
  2.6 0.1 broadcast_in_dim.17.refs_4_
  2.6 0.0 copy-done.4
  2.6 0.2 compare_reduce_fusion
  2.8 0.1 select_n.44
  2.9 0.1 broadcast_bitcast_fusion.refs_5_
  3.0 0.0 copy-done
  3.0 79.9 %shard_map.73 = bf16[8,128,128]{2,1,0:T(8,128)(2,1)S(1)} custom-call(bf16[8,128,128]{2,1,0:T(8,128)(2,1)S(1)} %copy-done, bf16[4,2,384,128]{3,2,1,0:T(8,128)(2,1)S(1)} %bitcast.13, bf16[4,2,16,128]{3,2,1,0:T(8,128)(2,1)S(1)} %maximum_bitcast_fusion.1.refs_2_, s32[8,128]{1,0:T(8,128)S(1)} %broadcast_in_dim.16.refs_3_, ...), custom_call_target="tpu_custom_call" | custom-call | flops 3355443200 | bytes 1310720 | tf_op jit(solution)/shard_map/pallas_call | solution.py:421
  82.9 0.7 copy.17
  (7 shorter events, 0.0 us)
Async XLA Ops:
  1.7 0.7 copy-start.1
  1.7 0.7 copy-start.2
  1.7 0.7 copy-start.3
  1.7 0.9 %copy-start.4 = (s32[32]{0:T(128)S(1)}, s32[32]{0:T(128)}, u32[]{:S(2)}) copy-start(s32[32]{0:T(128)} %param.13) | copy-start | bytes 388
  1.9 1.1 %copy-start = (bf16[8,128,128]{2,1,0:T(8,128)(2,1)S(1)}, bf16[8,128,128]{2,1,0:T(8,128)(2,1)}, u32[]{:S(2)}) copy-start(bf16[8,128,128]{2,1,0:T(8,128)(2,1)} %refs_0_.1) | copy-start | bytes 786436

commit v2 on v1

--- a/solution.py
+++ b/solution.py
@@ -9,7 +9,9 @@
 
 MESH = pl.DeviceIdType.MESH
 NEG = -1e30
-DELAY = 2
+DELAY = 3
+OWN_DELAY = 5
+SLOTS = 6
 
 
 def split_ctx(n):
@@ -135,16 +137,19 @@
         pl.semaphore_signal(barrier, inc=1, device_id=(z * B + grp(d), k), device_id_type=MESH)
     pl.semaphore_wait(barrier, K - 1 + A - 1 + B - 1)
 
-    for h in range(H):
-        for d in range(1, K):
-            q_x(h, d).start()
-        q_loc(h).start()
+    def kv_send(h):
         for d1 in range(1, B1):
             kv_far(h, d1).start()
         for d2 in range(1, B2):
             kv_near(h, d2).start()
         kv_loc(h).start()
+
+    for h in range(H):
+        for d in range(1, K):
+            q_x(h, d).start()
+        q_loc(h).start()
         if h == 0:
+            kv_send(h)
             for d in range(1, B):
                 n_out(d).start()
                 pk_out(d).start()
@@ -154,7 +159,7 @@
             pkbuf[g] = posk[...]
             pqbuf[z] = posq[...]
 
-    for h in range(H):
+    def q_own(h):
         q_loc(h).wait()
         for d in range(1, K):
             q_x_in(h, d).wait_recv()
@@ -187,6 +192,10 @@
     def kv_stage1(h):
         for d1 in range(1, B1):
             kv_in(h, ((b1 + B1 - d1) % B1) * B2 + b2).wait_recv()
+            if d1 == B1 - 1:
+                @pl.when(h + 2 < H)
+                def _():
+                    kv_send(h + 2)
             for d2 in range(1, B2):
                 kv_pass(h, d1, d2).start()
 
@@ -196,6 +205,10 @@
             for d1 in range(B1):
                 kv_in(h, ((b1 + B1 - d1) % B1) * B2 + (b2 + B2 - d2) % B2).wait_recv()
 
+    q_own(0)
+    if H > 1:
+        kv_send(1)
+        q_own(1)
     for d in range(1, A - 1):
         q_forward(0, d)
     kv_stage1(0)
@@ -280,6 +293,10 @@
             def _():
                 kv_stage2(h)
 
+                @pl.when(h + 2 < H)
+                def _():
+                    q_own(h + 2)
+
             @pl.when(h + 1 < H)
             def _():
                 for d in range(1, A):
@@ -291,39 +308,53 @@
                 def _():
                     kv_stage1(h + 1)
 
-            attend(h, order(j), s % (DELAY + 1))
-
-        @pl.when(s >= DELAY)
+            o, slot = order(j), s % SLOTS
+            attend(h, o, slot)
+
+            @pl.when((o > z) & (z == 0))
+            def _():
+                emit(h, o, slot, o_right(h, o))
+
+            @pl.when((o < z) & (z == A - 1))
+            def _():
+                emit(h, o, slot, o_left(h, o))
+
+        @pl.when((s >= DELAY) & (s < steps + DELAY))
         def _():
             t = s - DELAY
-            h, o, slot = t // A, order(t % A), t % (DELAY + 1)
-
-            @pl.when((o >= z) & (z > 0))
+            h, o, slot = t // A, order(t % A), t % SLOTS
+
+            @pl.when((o > z) & (z > 0))
             def _():
                 merge(h, o, slot, o_right(h, o), in_l, st_l)
-
-            @pl.when((o <= z) & (z < A - 1))
+                emit(h, o, slot, o_right(h, o))
+
+            @pl.when((o < z) & (z < A - 1))
             def _():
                 merge(h, o, slot, o_left(h, o), in_r, st_r)
-
-            @pl.when(o > z)
-            def _():
-                emit(h, o, slot, o_right(h, o))
-
-            @pl.when(o < z)
-            def _():
                 emit(h, o, slot, o_left(h, o))
 
-            @pl.when(o == z)
-            def _():
-                fin[h] = pbuf[slot].astype(jnp.bfloat16).reshape(T, G, 128)
-                for d in range(1, K):
-                    out_x(h, d).start()
-                out[:, heads(k, h), :] = fin[h, toks(k)]
+        @pl.when((s >= OWN_DELAY) & ((s - OWN_DELAY) % A == A - 1))
+        def _():
+            t = s - OWN_DELAY
+            h, slot = t // A, t % SLOTS
+
+            @pl.when(z > 0)
+            def _():
+                merge(h, z, slot, o_right(h, z), in_l, st_l)
+
+            @pl.when(z < A - 1)
+            def _():
+                merge(h, z, slot, o_left(h, z), in_r, st_r)
+
+            fin[h] = pbuf[slot].astype(jnp.bfloat16).reshape(T, G, 128)
+            for d in range(1, K):
+                out_x(h, d).start()
+            out[:, heads(k, h), :] = fin[h, toks(k)]
 
         return carry
 
-    lax.fori_loop(0, steps + DELAY, step, 0)
+    lax.fori_loop(0, steps + OWN_DELAY, step, 0)
 
     for d in range(1, B):
         n_out(d).wait_send()
@@ -404,7 +435,7 @@
         scratch = [
             V((H, A, T, G, width), bf), V((H, B, 2, SL, width), bf), V((B, H, 2, T, width), bf),
             V((B, 8, 128), i32), V((A, T, 128), i32), V((R, B * SL), f32),
-            V((DELAY + 1, R, 128), f32), V((DELAY + 1, R, 128), f32),
+            V((SLOTS, R, 128), f32), V((SLOTS, R, 128), f32),
             V((H, A, R, 128), bf), V((H, A, R // 16, 128), f32),
             V((H, A, R, 128), bf), V((H, A, R // 16, 128), f32),
             V((H, A, R, 128), bf), V((H, A, R // 16, 128), f32),

time: 83.8 us -> 67.5 us (0.81)
  Pallas kernels: 79.9 us -> 63.5 us
    pallas_call x1, Pallas kernels: 79.9 us -> 63.5 us  [body(): pl.pallas_call(lambda *refs: kernel(dims, *refs), out_shape=jax.ShapeDtyp...]
where the time goes in v2:
time: 67.5 us; the launch traced here: 67.3 us
  Pallas kernels  63.5 us (94%)
  other arithmetic  1.91 us (3%)
  local copies, waits for them, and re-layouts  1.73 us (3%)
    pallas_call x1, Pallas kernels, body(): pl.pallas_call(lambda *refs: kernel(dims, *refs), out_shape=jax.ShapeDtyp...  63.5 us
    transpose x1, other arithmetic, body(): jnp.stack([hist_keys, hist_values]).transpose(3, 0, 1, 2, 4)  1.7 us

profile of v2, /device:TPU:0, one launch (start us, length us, event | category | flops | bytes accessed | tf_op | source)
XLA Modules:
  0.0 67.3 jit_solution(13033029563045838834)
XLA Ops:
  0.0 1.7 %maximum_bitcast_fusion = bf16[4,2,3,128,128]{4,0,3,2,1:T(4,128)(2,1)S(1)} fusion(bf16[1,3,128,4,128]{4,3,2,1,0:T(4,128)(2,1)} %bitcast.14, bf16[1,3,128,4,128]{4,3,2,1,0:T(4,128)(2,1)} %bitcast.15), kind=kLoop, calls=%fused_computation | loop fusion | flops 393216 | bytes 1572864 | tf_op jit(solution)/shard_map/transpose | solution.py:419
  1.7 0.0 copy-start.1
  1.7 0.0 copy-start.2
  1.7 0.0 copy-start.3
  1.7 0.0 copy-start.4
  1.8 0.2 copy.11
  1.9 0.0 copy-start
  1.9 0.5 copy-done.1
  2.4 0.0 copy-done.2
  2.5 0.0 copy-done.3
  2.5 0.1 tile.10
  2.6 0.1 broadcast_in_dim.17.refs_4_
  2.6 0.0 copy-done.4
  2.6 0.2 compare_reduce_fusion
  2.8 0.1 select_n.44
  2.9 0.1 broadcast_bitcast_fusion.refs_5_
  3.0 0.0 copy-done
  3.0 63.5 %shard_map.73 = bf16[8,128,128]{2,1,0:T(8,128)(2,1)S(1)} custom-call(bf16[8,128,128]{2,1,0:T(8,128)(2,1)S(1)} %copy-done, bf16[4,2,384,128]{3,2,1,0:T(8,128)(2,1)S(1)} %bitcast.13, bf16[4,2,16,128]{3,2,1,0:T(8,128)(2,1)S(1)} %maximum_bitcast_fusion.1.refs_2_, s32[8,128]{1,0:T(8,128)S(1)} %broadcast_in_dim.16.refs_3_, ...), custom_call_target="tpu_custom_call" | custom-call | flops 3355443200 | bytes 1310720 | tf_op jit(solution)/shard_map/pallas_call | solution.py:452
  66.5 0.7 %copy.17 = bf16[8,128,128]{2,1,0:T(8,128)(2,1)} copy(bf16[8,128,128]{2,1,0:T(8,128)(2,1)S(1)} %shard_map.73) | data formatting | bytes 524288
  (7 shorter events, 0.0 us)
Async XLA Ops:
  1.7 0.7 %copy-start.1 = (bf16[16,4,128]{2,1,0:T(4,128)(2,1)S(1)}, bf16[16,4,128]{2,1,0:T(4,128)(2,1)}, u32[]{:S(2)}) copy-start(bf16[16,4,128]{2,1,0:T(4,128)(2,1)} %param.9) | copy-start | bytes 49156
  1.7 0.7 %copy-start.2 = (bf16[16,4,128]{2,1,0:T(4,128)(2,1)S(1)}, bf16[16,4,128]{2,1,0:T(4,128)(2,1)}, u32[]{:S(2)}) copy-start(bf16[16,4,128]{2,1,0:T(4,128)(2,1)} %param.8) | copy-start | bytes 49156
  1.7 0.7 %copy-start.3 = (s32[16]{0:T(128)S(1)}, s32[16]{0:T(128)}, u32[]{:S(2)}) copy-start(s32[16]{0:T(128)} %param.10) | copy-start | bytes 196
  1.7 0.9 %copy-start.4 = (s32[32]{0:T(128)S(1)}, s32[32]{0:T(128)}, u32[]{:S(2)}) copy-start(s32[32]{0:T(128)} %param.13) | copy-start | bytes 388
  1.9 1.1 %copy-start = (bf16[8,128,128]{2,1,0:T(8,128)(2,1)S(1)}, bf16[8,128,128]{2,1,0:T(8,128)(2,1)}, u32[]{:S(2)}) copy-start(bf16[8,128,128]{2,1,0:T(8,128)(2,1)} %refs_0_.1) | copy-start | bytes 786436

commit v3 on v2

--- a/solution.py
+++ b/solution.py
@@ -9,9 +9,8 @@
 
 MESH = pl.DeviceIdType.MESH
 NEG = -1e30
-DELAY = 3
-OWN_DELAY = 5
-SLOTS = 6
+FIRST_DELAY = 4
+HOP_DELAY = 2
 
 
 def split_ctx(n):
@@ -209,11 +208,10 @@
     if H > 1:
         kv_send(1)
         q_own(1)
-    for d in range(1, A - 1):
-        q_forward(0, d)
+    if H == 1:
+        for d in range(1, A):
+            q_forward(0, d)
     kv_stage1(0)
-    if A > 1:
-        q_forward(0, A - 1)
     pltpu.make_async_copy(new, nbuf.at[g], loc_n).wait()
     for d in range(1, B):
         n_in(d).wait_recv()
@@ -283,6 +281,9 @@
             cp.start()
 
     steps = H * A
+    from_left = FIRST_DELAY + HOP_DELAY * (z - 1)
+    from_right = FIRST_DELAY + HOP_DELAY * (A - 2 - z)
+    own_delay = FIRST_DELAY + HOP_DELAY * (A - 2)
 
     def step(s, carry):
         @pl.when(s < steps)
@@ -297,18 +298,21 @@
                 def _():
                     q_own(h + 2)
 
-            @pl.when(h + 1 < H)
-            def _():
-                for d in range(1, A):
-                    @pl.when(j == d - 1)
-                    def _():
-                        q_forward(h + 1, d)
-
-                @pl.when(j == A - 1)
+            for d in range(1, A):
+                @pl.when((j == d) & (h == 0) & (H > 1))
                 def _():
-                    kv_stage1(h + 1)
-
-            o, slot = order(j), s % SLOTS
+                    q_forward(0, d)
+
+                @pl.when((j == d) & (h + 1 < H))
+                def _():
+                    q_forward(h + 1, d)
+
+            @pl.when((h + 1 < H) & (j == max(A - 2, 0)))
+            def _():
+                kv_stage1(h + 1)
+
+            o = order(jnp.where((h == 0) & (H > 1), A - 1 - j, j))
+            slot = h * A + o
             attend(h, o, slot)
 
             @pl.when((o > z) & (z == 0))
@@ -319,25 +323,34 @@
             def _():
                 emit(h, o, slot, o_left(h, o))
 
-        @pl.when((s >= DELAY) & (s < steps + DELAY))
-        def _():
-            t = s - DELAY
-            h, o, slot = t // A, order(t % A), t % SLOTS
-
-            @pl.when((o > z) & (z > 0))
-            def _():
-                merge(h, o, slot, o_right(h, o), in_l, st_l)
-                emit(h, o, slot, o_right(h, o))
-
-            @pl.when((o < z) & (z < A - 1))
-            def _():
-                merge(h, o, slot, o_left(h, o), in_r, st_r)
-                emit(h, o, slot, o_left(h, o))
-
-        @pl.when((s >= OWN_DELAY) & ((s - OWN_DELAY) % A == A - 1))
-        def _():
-            t = s - OWN_DELAY
-            h, slot = t // A, t % SLOTS
+        tr = s - from_left
+
+        @pl.when((z > 0) & (tr >= 0) & (tr < steps))
+        def _():
+            h, o = tr // A, order(tr % A)
+
+            @pl.when(o > z)
+            def _():
+                merge(h, o, h * A + o, o_right(h, o), in_l, st_l)
+                emit(h, o, h * A + o, o_right(h, o))
+
+        tl = s - from_right
+
+        @pl.when((z < A - 1) & (tl >= 0) & (tl < steps))
+        def _():
+            h, o = tl // A, order(tl % A)
+
+            @pl.when(o < z)
+            def _():
+                merge(h, o, h * A + o, o_left(h, o), in_r, st_r)
+                emit(h, o, h * A + o, o_left(h, o))
+
+        to = s - own_delay
+
+        @pl.when((to >= 0) & (to % A == A - 1))
+        def _():
+            h = to // A
+            slot = h * A + z
 
             @pl.when(z > 0)
             def _():
@@ -354,7 +367,7 @@
 
         return carry
 
-    lax.fori_loop(0, steps + OWN_DELAY, step, 0)
+    lax.fori_loop(0, steps + own_delay, step, 0)
 
     for d in range(1, B):
         n_out(d).wait_send()
@@ -435,7 +448,7 @@
         scratch = [
             V((H, A, T, G, width), bf), V((H, B, 2, SL, width), bf), V((B, H, 2, T, width), bf),
             V((B, 8, 128), i32), V((A, T, 128), i32), V((R, B * SL), f32),
-            V((SLOTS, R, 128), f32), V((SLOTS, R, 128), f32),
+            V((H * A, R, 128), f32), V((H * A, R, 128), f32),
             V((H, A, R, 128), bf), V((H, A, R // 16, 128), f32),
             V((H, A, R, 128), bf), V((H, A, R // 16, 128), f32),
             V((H, A, R, 128), bf), V((H, A, R // 16, 128), f32),

time: 67.5 us -> 66.8 us (0.990)
  no operation moved by 1% of the time
where the time goes in v3:
time: 66.8 us; the launch traced here: 66.6 us
  Pallas kernels  62.9 us (94%)
  other arithmetic  1.91 us (3%)
  local copies, waits for them, and re-layouts  1.73 us (3%)
    pallas_call x1, Pallas kernels, body(): pl.pallas_call(lambda *refs: kernel(dims, *refs), out_shape=jax.ShapeDtyp...  62.9 us
    transpose x1, other arithmetic, body(): jnp.stack([hist_keys, hist_values]).transpose(3, 0, 1, 2, 4)  1.7 us

profile of v3, /device:TPU:0, one launch (start us, length us, event | category | flops | bytes accessed | tf_op | source)
XLA Modules:
  0.0 66.6 jit_solution(13412729702626432986)
XLA Ops:
  0.0 1.7 %maximum_bitcast_fusion = bf16[4,2,3,128,128]{4,0,3,2,1:T(4,128)(2,1)S(1)} fusion(bf16[1,3,128,4,128]{4,3,2,1,0:T(4,128)(2,1)} %bitcast.14, bf16[1,3,128,4,128]{4,3,2,1,0:T(4,128)(2,1)} %bitcast.15), kind=kLoop, calls=%fused_computation | loop fusion | flops 393216 | bytes 1572864 | tf_op jit(solution)/shard_map/transpose | solution.py:432
  1.7 0.0 copy-start.1
  1.7 0.0 copy-start.2
  1.7 0.0 copy-start.3
  1.7 0.0 copy-start.4
  1.8 0.2 copy.11
  1.9 0.0 copy-start
  1.9 0.5 copy-done.1
  2.4 0.0 copy-done.2
  2.5 0.0 copy-done.3
  2.5 0.1 tile.10
  2.6 0.1 broadcast_in_dim.17.refs_4_
  2.6 0.0 copy-done.4
  2.6 0.2 compare_reduce_fusion
  2.8 0.1 select_n.44
  2.9 0.1 broadcast_bitcast_fusion.refs_5_
  3.0 0.0 copy-done
  3.0 62.9 %shard_map.73 = bf16[8,128,128]{2,1,0:T(8,128)(2,1)S(1)} custom-call(bf16[8,128,128]{2,1,0:T(8,128)(2,1)S(1)} %copy-done, bf16[4,2,384,128]{3,2,1,0:T(8,128)(2,1)S(1)} %bitcast.13, bf16[4,2,16,128]{3,2,1,0:T(8,128)(2,1)S(1)} %maximum_bitcast_fusion.1.refs_2_, s32[8,128]{1,0:T(8,128)S(1)} %broadcast_in_dim.16.refs_3_, ...), custom_call_target="tpu_custom_call" | custom-call | flops 3355443200 | bytes 1310720 | tf_op jit(solution)/shard_map/pallas_call | solution.py:465
  65.9 0.7 %copy.17 = bf16[8,128,128]{2,1,0:T(8,128)(2,1)} copy(bf16[8,128,128]{2,1,0:T(8,128)(2,1)S(1)} %shard_map.73) | data formatting | bytes 524288
  (7 shorter events, 0.0 us)
Async XLA Ops:
  1.7 0.7 %copy-start.1 = (bf16[16,4,128]{2,1,0:T(4,128)(2,1)S(1)}, bf16[16,4,128]{2,1,0:T(4,128)(2,1)}, u32[]{:S(2)}) copy-start(bf16[16,4,128]{2,1,0:T(4,128)(2,1)} %param.9) | copy-start | bytes 49156
  1.7 0.7 %copy-start.2 = (bf16[16,4,128]{2,1,0:T(4,128)(2,1)S(1)}, bf16[16,4,128]{2,1,0:T(4,128)(2,1)}, u32[]{:S(2)}) copy-start(bf16[16,4,128]{2,1,0:T(4,128)(2,1)} %param.8) | copy-start | bytes 49156
  1.7 0.7 %copy-start.3 = (s32[16]{0:T(128)S(1)}, s32[16]{0:T(128)}, u32[]{:S(2)}) copy-start(s32[16]{0:T(128)} %param.10) | copy-start | bytes 196
  1.7 0.9 %copy-start.4 = (s32[32]{0:T(128)S(1)}, s32[32]{0:T(128)}, u32[]{:S(2)}) copy-start(s32[32]{0:T(128)} %param.13) | copy-start | bytes 388
  1.9 1.1 %copy-start = (bf16[8,128,128]{2,1,0:T(8,128)(2,1)S(1)}, bf16[8,128,128]{2,1,0:T(8,128)(2,1)}, u32[]{:S(2)}) copy-start(bf16[8,128,128]{2,1,0:T(8,128)(2,1)} %refs_0_.1) | copy-start | bytes 786436

commit v4 on v3

--- a/solution.py
+++ b/solution.py
@@ -21,7 +21,7 @@
 
 
 def kernel(dims, q_in, hist, new, posk, posq, bias, out,
-           qbuf, kvbuf, nbuf, pkbuf, pqbuf, sbuf, pbuf, lbuf, obuf, stbuf,
+           qbuf, kvbuf, nbuf, pkbuf, pqbuf, nvt, sbuf, pbuf, lbuf, obuf, stbuf,
            in_l, st_l, in_r, st_r, fin,
            loc_q, loc_kv, loc_n, qx_s, qx_r, qr_s, ql_s, qz_r, kv_s, kv_r, fw_s,
            n_s, n_r, pk_s, pk_r, pq_s, pq_r, or_s, ol_s, sr_s, sl_s,
@@ -229,54 +229,55 @@
 
     def attend(h, o, slot):
         q = qbuf[h, o].reshape(R, 128)
-        top = jnp.full((R, 128), NEG, jnp.float32)
+        fold = (-1, 8, R)
+        top = jnp.full((8, R), NEG, jnp.float32)
         for b in range(B):
-            s = lax.dot_general(q, kvbuf[h, b, 0], (((1,), (1,)), ((), ())),
+            s = lax.dot_general(kvbuf[h, b, 0], q, (((1,), (1,)), ((), ())),
                                 preferred_element_type=jnp.float32)
-            s = s * cc + bias[8 * b:8 * b + 1, :]
-            sbuf[:, b * SL:(b + 1) * SL] = s
+            sbuf[b * SL:(b + 1) * SL, :] = s
             for i in range(SL // 128):
-                top = jnp.maximum(top, s[:, i * 128:(i + 1) * 128])
+                part = jnp.max(s[i * 128:(i + 1) * 128].reshape(fold), axis=0)
+                top = jnp.maximum(top, part + bias[b * (SL // 128) + i])
         nk = nbuf[:, h, 0].reshape(B * T, 128)
-        sn = lax.dot_general(q, nk, (((1,), (1,)), ((), ())), preferred_element_type=jnp.float32)
-        pos_k = pkbuf[0]
-        for b in range(1, B):
-            pos_k = pos_k + pkbuf[b]
-        pos_q = jnp.broadcast_to(pqbuf[o][:, None, :], (T, G, 128)).reshape(R, 128)
-        seen = pos_k[0:1, :B * T] <= pos_q[:, :B * T]
-        sn = jnp.where(seen, sn * cc, NEG)
-        m = jnp.maximum(jnp.max(top, axis=-1, keepdims=True), jnp.max(sn, axis=-1, keepdims=True))
-        pn = jnp.exp2(sn - m)
-        nv = nbuf[:, h, 1].reshape(B * T, 128)
-        acc = jnp.dot(pn.astype(jnp.bfloat16), nv, preferred_element_type=jnp.float32)
-        total = jnp.zeros((R, 128), jnp.float32)
-        for b in range(B):
-            p = jnp.exp2(sbuf[:, b * SL:(b + 1) * SL] - m)
-            for i in range(SL // 128):
-                total = total + p[:, i * 128:(i + 1) * 128]
-            acc = acc + jnp.dot(p.astype(jnp.bfloat16), kvbuf[h, b, 1], preferred_element_type=jnp.float32)
-        denom = jnp.sum(total, axis=-1, keepdims=True) + jnp.sum(pn, axis=-1, keepdims=True)
+        sn = lax.dot_general(nk, q, (((1,), (1,)), ((), ())), preferred_element_type=jnp.float32)
+        pos_k = pkbuf[...].reshape(B * T, 128)
+        pos_k = jnp.concatenate([pos_k] * (R // 128), axis=1)
+        sn = jnp.where(pos_k <= pqbuf[o][0:1, :], sn, NEG)
+        top = jnp.maximum(top, jnp.max(sn.reshape(fold), axis=0))
+        m = jnp.max(top, axis=0, keepdims=True) * cc
+        pn = jnp.exp2(sn * cc - m)
+        total = jnp.sum(pn.reshape(fold), axis=0)
+        acc = jnp.dot(nvt[...], pn.astype(jnp.bfloat16), preferred_element_type=jnp.float32)
+        for b0 in range(0, B, 2):
+            ps, vs = [], []
+            for b in range(b0, min(b0 + 2, B)):
+                for i in range(SL // 128):
+                    row = b * SL + i * 128
+                    p = jnp.exp2(sbuf[row:row + 128, :] * cc - (m - bias[b * (SL // 128) + i]))
+                    total = total + jnp.sum(p.reshape(fold), axis=0)
+                    ps.append(p.astype(jnp.bfloat16))
+                    vs.append(kvbuf[h, b, 1, i * 128:(i + 1) * 128, :])
+            acc = acc + jnp.dot(jnp.concatenate(vs, axis=1), jnp.concatenate(ps, axis=0),
+                                preferred_element_type=jnp.float32)
+        denom = jnp.sum(total, axis=0, keepdims=True)
         pbuf[slot] = acc * (1.0 / denom)
-        lbuf[slot] = jnp.broadcast_to(m + jnp.log(denom) * math.log2(math.e), (R, 128))
+        lbuf[slot] = jnp.broadcast_to(m + jnp.log(denom) * math.log2(math.e), (8, R))
 
     def merge(h, o, slot, copies, data, stats):
         for cp in copies:
             cp.wait_recv()
         x = data[h, o].astype(jnp.float32)
-        for r in range(R // 128):
-            rows = slice(r * 128, (r + 1) * 128)
-            lx = jnp.transpose(jnp.broadcast_to(stats[h, o, 8 * r:8 * r + 1, :], (128, 128)))
-            lo = lbuf[slot, rows, :]
-            m = jnp.maximum(lx, lo)
-            wx, wo = jnp.exp2(lx - m), jnp.exp2(lo - m)
-            den = wx + wo
-            pbuf[slot, rows, :] = (wx * x[rows] + wo * pbuf[slot, rows, :]) * (1.0 / den)
-            lbuf[slot, rows, :] = m + jnp.log(den) * math.log2(math.e)
+        lx, lo = stats[h, o], lbuf[slot]
+        m = jnp.maximum(lx, lo)
+        wx, wo = jnp.exp2(lx - m), jnp.exp2(lo - m)
+        den = wx + wo
+        inv = 1.0 / den
+        pbuf[slot] = (wx * inv)[0:1] * x + (wo * inv)[0:1] * pbuf[slot]
+        lbuf[slot] = m + jnp.log(den) * math.log2(math.e)
 
     def emit(h, o, slot, copies):
         obuf[h, o] = pbuf[slot].astype(jnp.bfloat16)
-        for r in range(R // 128):
-            stbuf[h, o, 8 * r:8 * r + 8, :] = jnp.transpose(lbuf[slot, r * 128:(r + 1) * 128, :])[0:8, :]
+        stbuf[h, o] = lbuf[slot]
         for cp in copies:
             cp.start()
 
@@ -293,6 +294,8 @@
             @pl.when(j == 0)
             def _():
                 kv_stage2(h)
+                nv = nbuf[:, h, 1].reshape(B * T, 128).astype(jnp.float32)
+                nvt[...] = jnp.transpose(nv).astype(jnp.bfloat16)
 
                 @pl.when(h + 2 < H)
                 def _():
@@ -360,7 +363,7 @@
             def _():
                 merge(h, z, slot, o_left(h, z), in_r, st_r)
 
-            fin[h] = pbuf[slot].astype(jnp.bfloat16).reshape(T, G, 128)
+            fin[h] = jnp.transpose(pbuf[slot]).astype(jnp.bfloat16).reshape(T, G, 128)
             for d in range(1, K):
                 out_x(h, d).start()
             out[:, heads(k, h), :] = fin[h, toks(k)]
@@ -428,17 +431,16 @@
         SL = slots * page
         R = T * G
         c = lax.axis_index("ctx")
-        z, g = c // B, c % B
-        hist = jnp.stack([hist_keys, hist_values]).transpose(3, 0, 1, 2, 4).reshape(H, 2, SL, width)
+        z = c // B
+        keys = hist_keys.transpose(2, 0, 1, 3)
+        values = hist_values.transpose(2, 0, 3, 1)
+        hist = jnp.stack([keys, values], axis=1).reshape(H, 2, SL, width)
         new = jnp.stack([new_keys, new_values]).transpose(2, 0, 1, 3)
-        lane = jnp.arange(128)
-        row = jnp.where(lane // T == g, jnp.tile(new_positions, 128 // T), 0)
-        posk = jnp.broadcast_to(row[None, :], (8, 128))
-        posq = jnp.broadcast_to(new_positions[:, None], (T, 128))
+        posk = jnp.broadcast_to(new_positions[:, None], (T, 128))
+        posq = jnp.broadcast_to(jnp.repeat(new_positions, G)[None, :], (8, R))
         ids = z * B * slots + jnp.arange(B * slots, dtype=jnp.int32)
         live = jnp.any(page_slots[None, :] == ids[:, None], axis=1)
-        bias = jnp.where(live, 0.0, NEG).astype(jnp.float32).reshape(B, 1, slots, 1)
-        bias = jnp.broadcast_to(bias, (B, 8, slots, page)).reshape(B * 8, SL)
+        bias = jnp.where(live, 0.0, NEG).astype(jnp.float32)
 
         bf, f32, i32 = jnp.bfloat16, jnp.float32, jnp.int32
         V = pltpu.VMEM
@@ -447,11 +449,11 @@
         dims = (A, B, B2, K, H, T, T_loc, G, HPD, SL)
         scratch = [
             V((H, A, T, G, width), bf), V((H, B, 2, SL, width), bf), V((B, H, 2, T, width), bf),
-            V((B, 8, 128), i32), V((A, T, 128), i32), V((R, B * SL), f32),
-            V((H * A, R, 128), f32), V((H * A, R, 128), f32),
-            V((H, A, R, 128), bf), V((H, A, R // 16, 128), f32),
-            V((H, A, R, 128), bf), V((H, A, R // 16, 128), f32),
-            V((H, A, R, 128), bf), V((H, A, R // 16, 128), f32),
+            V((B, T, 128), i32), V((A, 8, R), i32), V((width, B * T), bf), V((B * SL, R), f32),
+            V((H * A, 128, R), f32), V((H * A, 8, R), f32),
+            V((H, A, 128, R), bf), V((H, A, 8, R), f32),
+            V((H, A, 128, R), bf), V((H, A, 8, R), f32),
+            V((H, A, 128, R), bf), V((H, A, 8, R), f32),
             V((H, T, G, width), bf),
             D((H,)), D((H,)), D, D((H, kp)), D((H, kp)), D((H, A)), D((H, A)), D((H, A)),
             D((H, B)), D((H, B)), D((H, max(B1 - 1, 1), max(B2 - 1, 1))),
@@ -465,7 +467,7 @@
         return pl.pallas_call(
             lambda *refs: kernel(dims, *refs),
             out_shape=jax.ShapeDtypeStruct((T_loc, QH, width), bf),
-            in_specs=[any_, any_, any_, vm, vm, vm],
+            in_specs=[any_, any_, any_, vm, vm, pl.BlockSpec(memory_space=pltpu.SMEM)],
             out_specs=vm,
             scratch_shapes=scratch,
             cost_estimate=pl.CostEstimate(flops=4 * work * width, bytes_accessed=2 * hist.size + 4 * queries.size, transcendentals=work),

time: 66.8 us -> 68.1 us (1.019)
  local copies, waits for them, and re-layouts: 1.73 us -> 4.23 us
  other arithmetic: 1.91 us -> 0.28 us
    transpose x1 -> x0, other arithmetic: 1.7 us -> none  [body(): jnp.stack([hist_keys, hist_values]).transpose(3, 0, 1, 2, 4)]
    unnamed x11 -> x13, local copies, waits for them, and re-layouts: 1.24 us -> 2.62 us
    transpose x1 -> x2, local copies, waits for them, and re-layouts: 0.16 us -> 1.38 us  [the longest x1 1.31 us: body(): values = hist_values.transpose(2, 0, 3, 1)]
where the time goes in v4:
time: 68.1 us; the launch traced here: 67.9 us
  Pallas kernels  63.3 us (93%)
  local copies, waits for them, and re-layouts  4.23 us (6%)
    pallas_call x1, Pallas kernels, body(): pl.pallas_call(lambda *refs: kernel(dims, *refs), out_shape=jax.ShapeDtyp...  63.3 us
    unnamed x13, local copies, waits for them, and re-layouts  2.62 us

profile of v4, /device:TPU:0, one launch (start us, length us, event | category | flops | bytes accessed | tf_op | source)
XLA Modules:
  0.0 67.9 jit_solution(6951015557376675909)
XLA Ops:
  0.0 0.0 copy-start.1
  0.0 1.3 %copy.13 = bf16[4,3,128,128]{3,2,1,0:T(8,128)(2,1)S(1)} copy(bf16[4,3,128,128]{2,0,3,1:T(4,128)(2,1)} %bitcast.12) | data formatting | bytes 786432 | tf_op jit(solution)/shard_map/transpose | solution.py:436
  1.3 0.0 copy-done.1
  1.3 0.1 copy.12
  1.4 0.0 copy-start.2
  1.4 0.0 copy-start.3
  1.4 0.0 copy-start
  1.4 0.1 pad_maximum_fusion.refs_1_
  1.5 0.6 copy-done.2
  2.1 0.0 copy-done.3
  2.1 0.0 copy-start.4
  2.2 0.6 copy-done.4
  2.8 0.1 broadcast_in_dim.26.refs_3_
  2.9 0.1 broadcast_in_dim.27
  2.9 0.1 broadcast_in_dim.28
  3.0 0.0 copy-start.5
  3.0 0.6 copy-done.5
  3.7 0.2 compare_reduce_fusion
  3.9 0.0 copy-done
  3.9 63.3 %shard_map.73 = bf16[8,128,128]{2,1,0:T(8,128)(2,1)S(1)} custom-call(bf16[8,128,128]{2,1,0:T(8,128)(2,1)S(1)} %copy-done, bf16[4,2,384,128]{3,2,1,0:T(8,128)(2,1)S(1)} %pad_maximum_fusion.refs_1_, bf16[4,2,16,128]{3,2,1,0:T(8,128)(2,1)S(1)} %maximum_bitcast_fusion.refs_2_, s32[16,128]{1,0:T(8,128)S(1)} %broadcast_in_dim.26.refs_3_, ...), custom_call_target="tpu_custom_call" | custom-call | flops 3355443200 | bytes 1310720 | tf_op jit(solution)/shard_map/pallas_call | solution.py:467
  67.2 0.7 %copy.19 = bf16[8,128,128]{2,1,0:T(8,128)(2,1)} copy(bf16[8,128,128]{2,1,0:T(8,128)(2,1)S(1)} %shard_map.73) | data formatting | bytes 524288
  (5 shorter events, 0.0 us)
Async XLA Ops:
  0.0 1.3 %copy-start.1 = (bf16[3,128,4,128]{3,2,1,0:T(4,128)(2,1)S(1)}, bf16[3,128,4,128]{3,2,1,0:T(4,128)(2,1)}, u32[]{:S(2)}) copy-start(bf16[3,128,4,128]{3,2,1,0:T(4,128)(2,1)} %param.11) | copy-start | bytes 1179652
  1.4 0.7 %copy-start.2 = (bf16[16,4,128]{2,1,0:T(4,128)(2,1)S(1)}, bf16[16,4,128]{2,1,0:T(4,128)(2,1)}, u32[]{:S(2)}) copy-start(bf16[16,4,128]{2,1,0:T(4,128)(2,1)} %param.9) | copy-start | bytes 49156
  1.4 0.7 %copy-start.3 = (bf16[16,4,128]{2,1,0:T(4,128)(2,1)S(1)}, bf16[16,4,128]{2,1,0:T(4,128)(2,1)}, u32[]{:S(2)}) copy-start(bf16[16,4,128]{2,1,0:T(4,128)(2,1)} %param.8) | copy-start | bytes 49156
  1.4 2.5 %copy-start = (bf16[8,128,128]{2,1,0:T(8,128)(2,1)S(1)}, bf16[8,128,128]{2,1,0:T(8,128)(2,1)}, u32[]{:S(2)}) copy-start(bf16[8,128,128]{2,1,0:T(8,128)(2,1)} %refs_0_.1) | copy-start | bytes 786436
  2.1 0.7 copy-start.4
  3.0 0.7 copy-start.5

commit v5 on v4

--- a/solution.py
+++ b/solution.py
@@ -20,8 +20,8 @@
     return rows, group, pair
 
 
-def kernel(dims, q_in, hist, new, posk, posq, bias, out,
-           qbuf, kvbuf, nbuf, pkbuf, pqbuf, nvt, sbuf, pbuf, lbuf, obuf, stbuf,
+def kernel(dims, q_in, hist, new, pos, pages, out,
+           qbuf, kvbuf, nbuf, pkbuf, pqbuf, bias, nvt, sbuf, pbuf, lbuf, obuf, stbuf,
            in_l, st_l, in_r, st_r, fin,
            loc_q, loc_kv, loc_n, qx_s, qx_r, qr_s, ql_s, qz_r, kv_s, kv_r, fw_s,
            n_s, n_r, pk_s, pk_r, pq_s, pq_r, or_s, ol_s, sr_s, sl_s,
@@ -92,10 +92,10 @@
         return remote(new, nbuf.at[g], n_s.at[d - 1], n_r.at[d - 1], (z * B + grp(d), k))
 
     def pk_out(d):
-        return remote(posk, pkbuf.at[g], pk_s.at[d - 1], pk_r.at[d - 1], (z * B + grp(d), k))
+        return remote(pkbuf.at[g], pkbuf.at[g], pk_s.at[d - 1], pk_r.at[d - 1], (z * B + grp(d), k))
 
     def pq_out(d):
-        return remote(posq, pqbuf.at[z], pq_s.at[d - 1], pq_r.at[d - 1], (((z + d) % A) * B + g, k))
+        return remote(pqbuf.at[z], pqbuf.at[z], pq_s.at[d - 1], pq_r.at[d - 1], (((z + d) % A) * B + g, k))
 
     def n_in(d):
         src = nbuf.at[(g + B - d) % B]
@@ -111,11 +111,11 @@
 
     def o_right(h, o):
         return (remote(obuf.at[h, o], in_l.at[h, o], or_s.at[h, o], ol_r.at[h, o], (c + B, k)),
-                remote(stbuf.at[h, o], st_l.at[h, o], sr_s.at[h, o], tl_r.at[h, o], (c + B, k)))
+                remote(stbuf.at[h, o, 0:1], st_l.at[h, o, 0:1], sr_s.at[h, o], tl_r.at[h, o], (c + B, k)))
 
     def o_left(h, o):
         return (remote(obuf.at[h, o], in_r.at[h, o], ol_s.at[h, o], or_r.at[h, o], (c - B, k)),
-                remote(stbuf.at[h, o], st_r.at[h, o], sl_s.at[h, o], tr_r.at[h, o], (c - B, k)))
+                remote(stbuf.at[h, o, 0:1], st_r.at[h, o, 0:1], sl_s.at[h, o], tr_r.at[h, o], (c - B, k)))
 
     def out_x(h, d):
         kk = (k + d) % K
@@ -126,6 +126,16 @@
         kk = (k + K - d) % K
         dst = out.at[:, heads(kk, h), :]
         return remote(fin.at[h, toks(kk)], dst, ox_s.at[h, d - 1], ox_r.at[h, d - 1], (c, kk))
+
+    def iota(shape, axis):
+        return lax.broadcasted_iota(jnp.int32, shape, axis)
+
+    row = jnp.broadcast_to(pos[...].astype(jnp.float32), (T, T))
+    column = jnp.sum(jnp.where(iota((T, T), 0) == iota((T, T), 1), row, 0.0), axis=1, keepdims=True)
+    pkbuf[g] = jnp.broadcast_to(column, (T, 128)).astype(jnp.int32)
+    own = iota((T, R), 0) == iota((T, R), 1) // G
+    spread = jnp.sum(jnp.where(own, jnp.broadcast_to(column, (T, R)), 0.0), axis=0, keepdims=True)
+    pqbuf[z] = jnp.broadcast_to(spread, (8, R)).astype(jnp.int32)
 
     barrier = pltpu.get_barrier_semaphore()
     for d in range(1, K):
@@ -147,16 +157,14 @@
         for d in range(1, K):
             q_x(h, d).start()
         q_loc(h).start()
+        kv_send(h)
         if h == 0:
-            kv_send(h)
             for d in range(1, B):
                 n_out(d).start()
                 pk_out(d).start()
             for d in range(1, A):
                 pq_out(d).start()
             pltpu.make_async_copy(new, nbuf.at[g], loc_n).start()
-            pkbuf[g] = posk[...]
-            pqbuf[z] = posq[...]
 
     def q_own(h):
         q_loc(h).wait()
@@ -191,10 +199,6 @@
     def kv_stage1(h):
         for d1 in range(1, B1):
             kv_in(h, ((b1 + B1 - d1) % B1) * B2 + b2).wait_recv()
-            if d1 == B1 - 1:
-                @pl.when(h + 2 < H)
-                def _():
-                    kv_send(h + 2)
             for d2 in range(1, B2):
                 kv_pass(h, d1, d2).start()
 
@@ -204,9 +208,13 @@
             for d1 in range(B1):
                 kv_in(h, ((b1 + B1 - d1) % B1) * B2 + (b2 + B2 - d2) % B2).wait_recv()
 
+    for i in range(B * SL // 128):
+        hit = jnp.where(pages[...] == z * (B * SL // 128) + i, 1.0, 0.0)
+        hit = jnp.max(hit, axis=1, keepdims=True)
+        bias[i] = jnp.broadcast_to((1.0 - hit) * NEG, (8, R))
+
     q_own(0)
     if H > 1:
-        kv_send(1)
         q_own(1)
     if H == 1:
         for d in range(1, A):
@@ -253,7 +261,7 @@
             for b in range(b0, min(b0 + 2, B)):
                 for i in range(SL // 128):
                     row = b * SL + i * 128
-                    p = jnp.exp2(sbuf[row:row + 128, :] * cc - (m - bias[b * (SL // 128) + i]))
+                    p = jnp.exp2(sbuf[row:row + 128, :] * cc - (m - bias[b * (SL // 128) + i, 0:1, :]))
                     total = total + jnp.sum(p.reshape(fold), axis=0)
                     ps.append(p.astype(jnp.bfloat16))
                     vs.append(kvbuf[h, b, 1, i * 128:(i + 1) * 128, :])
@@ -267,13 +275,13 @@
         for cp in copies:
             cp.wait_recv()
         x = data[h, o].astype(jnp.float32)
-        lx, lo = stats[h, o], lbuf[slot]
+        lx, lo = stats[h, o, 0:1, :], lbuf[slot, 0:1, :]
         m = jnp.maximum(lx, lo)
         wx, wo = jnp.exp2(lx - m), jnp.exp2(lo - m)
         den = wx + wo
         inv = 1.0 / den
-        pbuf[slot] = (wx * inv)[0:1] * x + (wo * inv)[0:1] * pbuf[slot]
-        lbuf[slot] = m + jnp.log(den) * math.log2(math.e)
+        pbuf[slot] = (wx * inv) * x + (wo * inv) * pbuf[slot]
+        lbuf[slot] = jnp.broadcast_to(m + jnp.log(den) * math.log2(math.e), (8, R))
 
     def emit(h, o, slot, copies):
         obuf[h, o] = pbuf[slot].astype(jnp.bfloat16)
@@ -430,17 +438,10 @@
         slots, page = hist_keys.shape[:2]
         SL = slots * page
         R = T * G
-        c = lax.axis_index("ctx")
-        z = c // B
         keys = hist_keys.transpose(2, 0, 1, 3)
         values = hist_values.transpose(2, 0, 3, 1)
         hist = jnp.stack([keys, values], axis=1).reshape(H, 2, SL, width)
         new = jnp.stack([new_keys, new_values]).transpose(2, 0, 1, 3)
-        posk = jnp.broadcast_to(new_positions[:, None], (T, 128))
-        posq = jnp.broadcast_to(jnp.repeat(new_positions, G)[None, :], (8, R))
-        ids = z * B * slots + jnp.arange(B * slots, dtype=jnp.int32)
-        live = jnp.any(page_slots[None, :] == ids[:, None], axis=1)
-        bias = jnp.where(live, 0.0, NEG).astype(jnp.float32)
 
         bf, f32, i32 = jnp.bfloat16, jnp.float32, jnp.int32
         V = pltpu.VMEM
@@ -449,7 +450,7 @@
         dims = (A, B, B2, K, H, T, T_loc, G, HPD, SL)
         scratch = [
             V((H, A, T, G, width), bf), V((H, B, 2, SL, width), bf), V((B, H, 2, T, width), bf),
-            V((B, T, 128), i32), V((A, 8, R), i32), V((width, B * T), bf), V((B * SL, R), f32),
+            V((B, T, 128), i32), V((A, 8, R), i32), V((B * slots, 8, R), f32), V((width, B * T), bf), V((B * SL, R), f32),
             V((H * A, 128, R), f32), V((H * A, 8, R), f32),
             V((H, A, 128, R), bf), V((H, A, 8, R), f32),
             V((H, A, 128, R), bf), V((H, A, 8, R), f32),
@@ -467,13 +468,13 @@
         return pl.pallas_call(
             lambda *refs: kernel(dims, *refs),
             out_shape=jax.ShapeDtypeStruct((T_loc, QH, width), bf),
-            in_specs=[any_, any_, any_, vm, vm, pl.BlockSpec(memory_space=pltpu.SMEM)],
+            in_specs=[any_, any_, any_, vm, vm],
             out_specs=vm,
             scratch_shapes=scratch,
             cost_estimate=pl.CostEstimate(flops=4 * work * width, bytes_accessed=2 * hist.size + 4 * queries.size, transcendentals=work),
             compiler_params=pltpu.CompilerParams(
                 collective_id=0, has_side_effects=True, vmem_limit_bytes=40 * 1024 * 1024),
-        )(queries, hist, new, posk, posq, bias)
+        )(queries, hist, new, new_positions[None, :], page_slots[None, :])
 
     in_specs = (
         P(("ctx", "kvh"), None, None), P("ctx", "kvh", None), P("ctx", "kvh", None), P("ctx"),

time: 68.1 us -> 66 us (0.969)
  Pallas kernels: 63.3 us -> 62.2 us
  local copies, waits for them, and re-layouts: 4.23 us -> 3.4 us
    pallas_call x1, Pallas kernels: 63.3 us -> 62.2 us  [body(): pl.pallas_call(lambda *refs: kernel(dims, *refs), out_shape=jax.ShapeDtyp...]
where the time goes in v5:
time: 66 us; the launch traced here: 65.8 us
  Pallas kernels  62.2 us (94%)
  local copies, waits for them, and re-layouts  3.4 us (5%)
    pallas_call x1, Pallas kernels, body(): pl.pallas_call(lambda *refs: kernel(dims, *refs), out_shape=jax.ShapeDtyp...  62.2 us
    unnamed x13, local copies, waits for them, and re-layouts  2.01 us

profile of v5, /device:TPU:0, one launch (start us, length us, event | category | flops | bytes accessed | tf_op | source)
XLA Modules:
  0.0 65.8 jit_solution(11439081214633536519)
XLA Ops:
  0.0 0.0 copy-start.3
  0.0 1.3 %copy.9 = bf16[4,3,128,128]{3,2,1,0:T(8,128)(2,1)S(1)} copy(bf16[4,3,128,128]{2,0,3,1:T(4,128)(2,1)} %bitcast.16) | data formatting | bytes 786432 | tf_op jit(solution)/shard_map/transpose | solution.py:442
  1.3 0.0 copy-done.3
  1.3 0.1 copy.8
  1.4 0.0 copy-start.4
  1.4 0.0 copy-start.5
  1.4 0.0 copy-start
  1.4 0.1 pad_maximum_fusion.refs_1_
  1.5 0.6 copy-done.4
  2.1 0.0 copy-done.5
  2.2 0.0 copy-start.1
  2.2 0.0 copy-start.2
  2.2 0.2 copy-done
  2.4 0.4 copy-done.1
  2.8 0.0 copy-done.2
  2.9 62.2 %shard_map.73 = bf16[8,128,128]{2,1,0:T(8,128)(2,1)S(1)} custom-call(bf16[8,128,128]{2,1,0:T(8,128)(2,1)S(1)} %copy-done, bf16[4,2,384,128]{3,2,1,0:T(8,128)(2,1)S(1)} %pad_maximum_fusion.refs_1_, bf16[4,2,16,128]{3,2,1,0:T(8,128)(2,1)S(1)} %maximum_bitcast_fusion.refs_2_, s32[1,16]{1,0:T(1,128)S(1)} %bitcast.12, s32[1,32]{1,0:T(1,128)S(1)} %bitcast.13), custom_call_target="tpu_custom_call" | custom-call | flops 3355443200 | bytes 1310720 | tf_op jit(solution)/shard_map/pallas_call | solution.py:468
  65.1 0.7 %copy.15 = bf16[8,128,128]{2,1,0:T(8,128)(2,1)} copy(bf16[8,128,128]{2,1,0:T(8,128)(2,1)S(1)} %shard_map.73) | data formatting | bytes 524288
  (2 shorter events, 0.0 us)
Async XLA Ops:
  0.0 1.3 %copy-start.3 = (bf16[3,128,4,128]{3,2,1,0:T(4,128)(2,1)S(1)}, bf16[3,128,4,128]{3,2,1,0:T(4,128)(2,1)}, u32[]{:S(2)}) copy-start(bf16[3,128,4,128]{3,2,1,0:T(4,128)(2,1)} %param.11) | copy-start | bytes 1179652
  1.4 0.7 %copy-start.4 = (bf16[16,4,128]{2,1,0:T(4,128)(2,1)S(1)}, bf16[16,4,128]{2,1,0:T(4,128)(2,1)}, u32[]{:S(2)}) copy-start(bf16[16,4,128]{2,1,0:T(4,128)(2,1)} %param.9) | copy-start | bytes 49156
  1.4 0.7 %copy-start.5 = (bf16[16,4,128]{2,1,0:T(4,128)(2,1)S(1)}, bf16[16,4,128]{2,1,0:T(4,128)(2,1)}, u32[]{:S(2)}) copy-start(bf16[16,4,128]{2,1,0:T(4,128)(2,1)} %param.8) | copy-start | bytes 49156
  1.4 1.0 %copy-start = (bf16[8,128,128]{2,1,0:T(8,128)(2,1)S(1)}, bf16[8,128,128]{2,1,0:T(8,128)(2,1)}, u32[]{:S(2)}) copy-start(bf16[8,128,128]{2,1,0:T(8,128)(2,1)} %refs_0_.1) | copy-start | bytes 786436
  2.2 0.7 %copy-start.1 = (s32[16]{0:T(128)S(1)}, s32[16]{0:T(128)}, u32[]{:S(2)}) copy-start(s32[16]{0:T(128)} %param.10) | copy-start | bytes 196
  2.2 0.7 %copy-start.2 = (s32[32]{0:T(128)S(1)}, s32[32]{0:T(128)}, u32[]{:S(2)}) copy-start(s32[32]{0:T(128)} %param.13) | copy-start | bytes 388

commit v6 on v5

--- a/solution.py
+++ b/solution.py
@@ -213,9 +213,8 @@
         hit = jnp.max(hit, axis=1, keepdims=True)
         bias[i] = jnp.broadcast_to((1.0 - hit) * NEG, (8, R))
 
-    q_own(0)
-    if H > 1:
-        q_own(1)
+    for h in range(H):
+        q_own(h)
     if H == 1:
         for d in range(1, A):
             q_forward(0, d)
@@ -235,14 +234,15 @@
         f = jnp.where(j < far, A - 1 - j, jnp.where(j < A - 1, j - far, zf))
         return jnp.where(low, f, A - 1 - f)
 
-    def attend(h, o, slot):
+    fold = (-1, 8, R)
+
+    def score(h, o, lane):
         q = qbuf[h, o].reshape(R, 128)
-        fold = (-1, 8, R)
         top = jnp.full((8, R), NEG, jnp.float32)
         for b in range(B):
             s = lax.dot_general(kvbuf[h, b, 0], q, (((1,), (1,)), ((), ())),
                                 preferred_element_type=jnp.float32)
-            sbuf[b * SL:(b + 1) * SL, :] = s
+            sbuf[lane, b * SL:(b + 1) * SL, :] = s
             for i in range(SL // 128):
                 part = jnp.max(s[i * 128:(i + 1) * 128].reshape(fold), axis=0)
                 top = jnp.maximum(top, part + bias[b * (SL // 128) + i])
@@ -252,7 +252,9 @@
         pos_k = jnp.concatenate([pos_k] * (R // 128), axis=1)
         sn = jnp.where(pos_k <= pqbuf[o][0:1, :], sn, NEG)
         top = jnp.maximum(top, jnp.max(sn.reshape(fold), axis=0))
-        m = jnp.max(top, axis=0, keepdims=True) * cc
+        return sn, jnp.max(top, axis=0, keepdims=True) * cc
+
+    def weigh(h, slot, lane, sn, m):
         pn = jnp.exp2(sn * cc - m)
         total = jnp.sum(pn.reshape(fold), axis=0)
         acc = jnp.dot(nvt[...], pn.astype(jnp.bfloat16), preferred_element_type=jnp.float32)
@@ -261,7 +263,7 @@
             for b in range(b0, min(b0 + 2, B)):
                 for i in range(SL // 128):
                     row = b * SL + i * 128
-                    p = jnp.exp2(sbuf[row:row + 128, :] * cc - (m - bias[b * (SL // 128) + i, 0:1, :]))
+                    p = jnp.exp2(sbuf[lane, row:row + 128, :] * cc - (m - bias[b * (SL // 128) + i, 0:1, :]))
                     total = total + jnp.sum(p.reshape(fold), axis=0)
                     ps.append(p.astype(jnp.bfloat16))
                     vs.append(kvbuf[h, b, 1, i * 128:(i + 1) * 128, :])
@@ -270,6 +272,11 @@
         denom = jnp.sum(total, axis=0, keepdims=True)
         pbuf[slot] = acc * (1.0 / denom)
         lbuf[slot] = jnp.broadcast_to(m + jnp.log(denom) * math.log2(math.e), (8, R))
+
+    def attend(h, owners):
+        found = [score(h, o, i) for i, o in enumerate(owners)]
+        for i, o in enumerate(owners):
+            weigh(h, h * A + o, i, *found[i])
 
     def merge(h, o, slot, copies, data, stats):
         for cp in copies:
@@ -290,6 +297,7 @@
             cp.start()
 
     steps = H * A
+    width = 2 if A % 2 == 0 else 1
     from_left = FIRST_DELAY + HOP_DELAY * (z - 1)
     from_right = FIRST_DELAY + HOP_DELAY * (A - 2 - z)
     own_delay = FIRST_DELAY + HOP_DELAY * (A - 2)
@@ -305,12 +313,8 @@
                 nv = nbuf[:, h, 1].reshape(B * T, 128).astype(jnp.float32)
                 nvt[...] = jnp.transpose(nv).astype(jnp.bfloat16)
 
-                @pl.when(h + 2 < H)
-                def _():
-                    q_own(h + 2)
-
             for d in range(1, A):
-                @pl.when((j == d) & (h == 0) & (H > 1))
+                @pl.when((j == d // width * width) & (h == 0) & (H > 1))
                 def _():
                     q_forward(0, d)
 
@@ -322,17 +326,21 @@
             def _():
                 kv_stage1(h + 1)
 
-            o = order(jnp.where((h == 0) & (H > 1), A - 1 - j, j))
-            slot = h * A + o
-            attend(h, o, slot)
-
-            @pl.when((o > z) & (z == 0))
-            def _():
-                emit(h, o, slot, o_right(h, o))
-
-            @pl.when((o < z) & (z == A - 1))
-            def _():
-                emit(h, o, slot, o_left(h, o))
+            first = (h == 0) & (H > 1)
+            owners = [order(jnp.where(first, A - 1 - j - i, j + i)) for i in range(width)]
+
+            @pl.when(j % width == 0)
+            def _():
+                attend(h, owners)
+
+                for o in owners:
+                    @pl.when((o > z) & (z == 0))
+                    def _():
+                        emit(h, o, h * A + o, o_right(h, o))
+
+                    @pl.when((o < z) & (z == A - 1))
+                    def _():
+                        emit(h, o, h * A + o, o_left(h, o))
 
         tr = s - from_left
 
@@ -450,7 +458,7 @@
         dims = (A, B, B2, K, H, T, T_loc, G, HPD, SL)
         scratch = [
             V((H, A, T, G, width), bf), V((H, B, 2, SL, width), bf), V((B, H, 2, T, width), bf),
-            V((B, T, 128), i32), V((A, 8, R), i32), V((B * slots, 8, R), f32), V((width, B * T), bf), V((B * SL, R), f32),
+            V((B, T, 128), i32), V((A, 8, R), i32), V((B * slots, 8, R), f32), V((width, B * T), bf), V((2, B * SL, R), f32),
             V((H * A, 128, R), f32), V((H * A, 8, R), f32),
             V((H, A, 128, R), bf), V((H, A, 8, R), f32),
             V((H, A, 128, R), bf), V((H, A, 8, R), f32),

time: 66 us -> 64.6 us (0.979)
  Pallas kernels: 62.2 us -> 60.8 us
    pallas_call x1, Pallas kernels: 62.2 us -> 60.8 us  [body(): pl.pallas_call(lambda *refs: kernel(dims, *refs), out_shape=jax.ShapeDtyp...]
where the time goes in v6:
time: 64.6 us; the launch traced here: 64.4 us
  Pallas kernels  60.8 us (94%)
  local copies, waits for them, and re-layouts  3.4 us (5%)
    pallas_call x1, Pallas kernels, body(): pl.pallas_call(lambda *refs: kernel(dims, *refs), out_shape=jax.ShapeDtyp...  60.8 us
    unnamed x13, local copies, waits for them, and re-layouts  2.01 us
    transpose x1, local copies, waits for them, and re-layouts, body(): values = hist_values.transpose(2, 0, 3, 1)  1.31 us

profile of v6, /device:TPU:0, one launch (start us, length us, event | category | flops | bytes accessed | tf_op | source)
XLA Modules:
  0.0 64.4 jit_solution(11265555509994390898)
XLA Ops:
  0.0 0.0 copy-start.3
  0.0 1.3 %copy.9 = bf16[4,3,128,128]{3,2,1,0:T(8,128)(2,1)S(1)} copy(bf16[4,3,128,128]{2,0,3,1:T(4,128)(2,1)} %bitcast.16) | data formatting | bytes 786432 | tf_op jit(solution)/shard_map/transpose | solution.py:450
  1.3 0.0 copy-done.3
  1.3 0.1 copy.8
  1.4 0.0 copy-start.4
  1.4 0.0 copy-start.5
  1.4 0.0 copy-start
  1.4 0.1 pad_maximum_fusion.refs_1_
  1.5 0.6 copy-done.4
  2.1 0.0 copy-done.5
  2.2 0.0 copy-start.1
  2.2 0.0 copy-start.2
  2.2 0.2 copy-done
  2.4 0.4 copy-done.1
  2.8 0.0 copy-done.2
  2.9 60.8 %shard_map.73 = bf16[8,128,128]{2,1,0:T(8,128)(2,1)S(1)} custom-call(bf16[8,128,128]{2,1,0:T(8,128)(2,1)S(1)} %copy-done, bf16[4,2,384,128]{3,2,1,0:T(8,128)(2,1)S(1)} %pad_maximum_fusion.refs_1_, bf16[4,2,16,128]{3,2,1,0:T(8,128)(2,1)S(1)} %maximum_bitcast_fusion.refs_2_, s32[1,16]{1,0:T(1,128)S(1)} %bitcast.12, s32[1,32]{1,0:T(1,128)S(1)} %bitcast.13), custom_call_target="tpu_custom_call" | custom-call | flops 3355443200 | bytes 1310720 | tf_op jit(solution)/shard_map/pallas_call | solution.py:476
  63.7 0.7 %copy.15 = bf16[8,128,128]{2,1,0:T(8,128)(2,1)} copy(bf16[8,128,128]{2,1,0:T(8,128)(2,1)S(1)} %shard_map.73) | data formatting | bytes 524288
  (2 shorter events, 0.0 us)
Async XLA Ops:
  0.0 1.3 %copy-start.3 = (bf16[3,128,4,128]{3,2,1,0:T(4,128)(2,1)S(1)}, bf16[3,128,4,128]{3,2,1,0:T(4,128)(2,1)}, u32[]{:S(2)}) copy-start(bf16[3,128,4,128]{3,2,1,0:T(4,128)(2,1)} %param.11) | copy-start | bytes 1179652
  1.4 0.7 %copy-start.4 = (bf16[16,4,128]{2,1,0:T(4,128)(2,1)S(1)}, bf16[16,4,128]{2,1,0:T(4,128)(2,1)}, u32[]{:S(2)}) copy-start(bf16[16,4,128]{2,1,0:T(4,128)(2,1)} %param.9) | copy-start | bytes 49156
  1.4 0.7 %copy-start.5 = (bf16[16,4,128]{2,1,0:T(4,128)(2,1)S(1)}, bf16[16,4,128]{2,1,0:T(4,128)(2,1)}, u32[]{:S(2)}) copy-start(bf16[16,4,128]{2,1,0:T(4,128)(2,1)} %param.8) | copy-start | bytes 49156
  1.4 1.0 %copy-start = (bf16[8,128,128]{2,1,0:T(8,128)(2,1)S(1)}, bf16[8,128,128]{2,1,0:T(8,128)(2,1)}, u32[]{:S(2)}) copy-start(bf16[8,128,128]{2,1,0:T(8,128)(2,1)} %refs_0_.1) | copy-start | bytes 786436
  2.2 0.7 %copy-start.1 = (s32[16]{0:T(128)S(1)}, s32[16]{0:T(128)}, u32[]{:S(2)}) copy-start(s32[16]{0:T(128)} %param.10) | copy-start | bytes 196
  2.2 0.7 %copy-start.2 = (s32[32]{0:T(128)S(1)}, s32[32]{0:T(128)}, u32[]{:S(2)}) copy-start(s32[32]{0:T(128)} %param.13) | copy-start | bytes 388

commit v7 on v6

--- a/solution.py
+++ b/solution.py
@@ -9,8 +9,8 @@
 
 MESH = pl.DeviceIdType.MESH
 NEG = -1e30
-FIRST_DELAY = 4
-HOP_DELAY = 2
+FIRST_DELAY = 3
+HOP_DELAY = 1
 
 
 def split_ctx(n):
@@ -20,11 +20,11 @@
     return rows, group, pair
 
 
-def kernel(dims, q_in, hist, new, pos, pages, out,
-           qbuf, kvbuf, nbuf, pkbuf, pqbuf, bias, nvt, sbuf, pbuf, lbuf, obuf, stbuf,
+def kernel(dims, q_in, hist, pos, pages, out,
+           qbuf, kvbuf, pkbuf, pqbuf, bias, nvt, sbuf, pbuf, lbuf, obuf, stbuf,
            in_l, st_l, in_r, st_r, fin,
-           loc_q, loc_kv, loc_n, qx_s, qx_r, qr_s, ql_s, qz_r, kv_s, kv_r, fw_s,
-           n_s, n_r, pk_s, pk_r, pq_s, pq_r, or_s, ol_s, sr_s, sl_s,
+           loc_q, loc_kv, qx_s, qx_r, qr_s, ql_s, qz_r, kv_s, kv_r, fw_s,
+           pk_s, pk_r, pq_s, pq_r, or_s, ol_s, sr_s, sl_s,
            ol_r, or_r, tl_r, tr_r, ox_s, ox_r):
     A, B, B2, K, H, T, T_loc, G, HPD, SL = dims
     B1 = B // B2
@@ -88,18 +88,11 @@
         to = z * B + b1 * B2 + (b2 + d2) % B2
         return remote(kvbuf.at[h, src], kvbuf.at[h, src], fw_s.at[h, d1 - 1, d2 - 1], kv_r.at[h, src], (to, k))
 
-    def n_out(d):
-        return remote(new, nbuf.at[g], n_s.at[d - 1], n_r.at[d - 1], (z * B + grp(d), k))
-
     def pk_out(d):
         return remote(pkbuf.at[g], pkbuf.at[g], pk_s.at[d - 1], pk_r.at[d - 1], (z * B + grp(d), k))
 
     def pq_out(d):
         return remote(pqbuf.at[z], pqbuf.at[z], pq_s.at[d - 1], pq_r.at[d - 1], (((z + d) % A) * B + g, k))
-
-    def n_in(d):
-        src = nbuf.at[(g + B - d) % B]
-        return remote(src, src, n_s.at[d - 1], n_r.at[d - 1], (c, k))
 
     def pk_in(d):
         src = pkbuf.at[(g + B - d) % B]
@@ -160,11 +153,9 @@
         kv_send(h)
         if h == 0:
             for d in range(1, B):
-                n_out(d).start()
                 pk_out(d).start()
             for d in range(1, A):
                 pq_out(d).start()
-            pltpu.make_async_copy(new, nbuf.at[g], loc_n).start()
 
     def q_own(h):
         q_loc(h).wait()
@@ -219,9 +210,7 @@
         for d in range(1, A):
             q_forward(0, d)
     kv_stage1(0)
-    pltpu.make_async_copy(new, nbuf.at[g], loc_n).wait()
     for d in range(1, B):
-        n_in(d).wait_recv()
         pk_in(d).wait_recv()
     for d in range(1, A):
         pq_in(d).wait_recv()
@@ -240,13 +229,13 @@
         q = qbuf[h, o].reshape(R, 128)
         top = jnp.full((8, R), NEG, jnp.float32)
         for b in range(B):
-            s = lax.dot_general(kvbuf[h, b, 0], q, (((1,), (1,)), ((), ())),
+            s = lax.dot_general(kvbuf[h, b, 0, :SL, :], q, (((1,), (1,)), ((), ())),
                                 preferred_element_type=jnp.float32)
             sbuf[lane, b * SL:(b + 1) * SL, :] = s
             for i in range(SL // 128):
                 part = jnp.max(s[i * 128:(i + 1) * 128].reshape(fold), axis=0)
                 top = jnp.maximum(top, part + bias[b * (SL // 128) + i])
-        nk = nbuf[:, h, 0].reshape(B * T, 128)
+        nk = kvbuf[h, :, 0, SL:SL + T, :].reshape(B * T, 128)
         sn = lax.dot_general(nk, q, (((1,), (1,)), ((), ())), preferred_element_type=jnp.float32)
         pos_k = pkbuf[...].reshape(B * T, 128)
         pos_k = jnp.concatenate([pos_k] * (R // 128), axis=1)
@@ -310,7 +299,7 @@
             @pl.when(j == 0)
             def _():
                 kv_stage2(h)
-                nv = nbuf[:, h, 1].reshape(B * T, 128).astype(jnp.float32)
+                nv = kvbuf[h, :, 1, SL:SL + T, :].reshape(B * T, 128).astype(jnp.float32)
                 nvt[...] = jnp.transpose(nv).astype(jnp.bfloat16)
 
             for d in range(1, A):
@@ -389,7 +378,6 @@
     lax.fori_loop(0, steps + own_delay, step, 0)
 
     for d in range(1, B):
-        n_out(d).wait_send()
         pk_out(d).wait_send()
     for d in range(1, A):
         pq_out(d).wait_send()
@@ -448,8 +436,9 @@
         R = T * G
         keys = hist_keys.transpose(2, 0, 1, 3)
         values = hist_values.transpose(2, 0, 3, 1)
+        new = jnp.stack([new_keys, new_values]).transpose(2, 0, 1, 3)
         hist = jnp.stack([keys, values], axis=1).reshape(H, 2, SL, width)
-        new = jnp.stack([new_keys, new_values]).transpose(2, 0, 1, 3)
+        hist = jnp.concatenate([hist, new], axis=2)
 
         bf, f32, i32 = jnp.bfloat16, jnp.float32, jnp.int32
         V = pltpu.VMEM
@@ -457,16 +446,16 @@
         kp, ap, bp = max(K - 1, 1), max(A - 1, 1), max(B - 1, 1)
         dims = (A, B, B2, K, H, T, T_loc, G, HPD, SL)
         scratch = [
-            V((H, A, T, G, width), bf), V((H, B, 2, SL, width), bf), V((B, H, 2, T, width), bf),
+            V((H, A, T, G, width), bf), V((H, B, 2, SL + T, width), bf),
             V((B, T, 128), i32), V((A, 8, R), i32), V((B * slots, 8, R), f32), V((width, B * T), bf), V((2, B * SL, R), f32),
             V((H * A, 128, R), f32), V((H * A, 8, R), f32),
             V((H, A, 128, R), bf), V((H, A, 8, R), f32),
             V((H, A, 128, R), bf), V((H, A, 8, R), f32),
             V((H, A, 128, R), bf), V((H, A, 8, R), f32),
             V((H, T, G, width), bf),
-            D((H,)), D((H,)), D, D((H, kp)), D((H, kp)), D((H, A)), D((H, A)), D((H, A)),
+            D((H,)), D((H,)), D((H, kp)), D((H, kp)), D((H, A)), D((H, A)), D((H, A)),
             D((H, B)), D((H, B)), D((H, max(B1 - 1, 1), max(B2 - 1, 1))),
-            D((bp,)), D((bp,)), D((bp,)), D((bp,)), D((ap,)), D((ap,)),
+            D((bp,)), D((bp,)), D((ap,)), D((ap,)),
             D((H, A)), D((H, A)), D((H, A)), D((H, A)),
             D((H, A)), D((H, A)), D((H, A)), D((H, A)), D((H, kp)), D((H, kp)),
         ]
@@ -476,13 +465,13 @@
         return pl.pallas_call(
             lambda *refs: kernel(dims, *refs),
             out_shape=jax.ShapeDtypeStruct((T_loc, QH, width), bf),
-            in_specs=[any_, any_, any_, vm, vm],
+            in_specs=[any_, any_, vm, vm],
             out_specs=vm,
             scratch_shapes=scratch,
             cost_estimate=pl.CostEstimate(flops=4 * work * width, bytes_accessed=2 * hist.size + 4 * queries.size, transcendentals=work),
             compiler_params=pltpu.CompilerParams(
                 collective_id=0, has_side_effects=True, vmem_limit_bytes=40 * 1024 * 1024),
-        )(queries, hist, new, new_positions[None, :], page_slots[None, :])
+        )(queries, hist, new_positions[None, :], page_slots[None, :])
 
     in_specs = (
         P(("ctx", "kvh"), None, None), P("ctx", "kvh", None), P("ctx", "kvh", None), P("ctx"),

time: 64.6 us -> 66.3 us (1.026)
  Pallas kernels: 60.8 us -> 62.3 us
    pallas_call x1, Pallas kernels: 60.8 us -> 62.3 us  [body(): pl.pallas_call(lambda *refs: kernel(dims, *refs), out_shape=jax.ShapeDtyp...]
    transpose x1, local copies, waits for them, and re-layouts: 1.31 us -> 0.29 us  [body(): values = hist_values.transpose(2, 0, 3, 1)]
    transpose x1, local copies, waits for them, and re-layouts: 0.07 us -> 1.06 us  [body(): keys = hist_keys.transpose(2, 0, 1, 3)]
    another operation x1, local copies, waits for them, and re-layouts: 0.01 us -> 0.79 us  [body(): new = jnp.stack([new_keys, new_values]).transpose(2, 0, 1, 3)]
    unnamed x13 -> x9, local copies, waits for them, and re-layouts: 2.01 us -> 1.58 us
where the time goes in v7:
time: 66.3 us; the launch traced here: 66.1 us
  Pallas kernels  62.3 us (94%)
  local copies, waits for them, and re-layouts  3.73 us (6%)
    pallas_call x1, Pallas kernels, body(): pl.pallas_call(lambda *refs: kernel(dims, *refs), out_shape=jax.ShapeDtyp...  62.3 us
    unnamed x9, local copies, waits for them, and re-layouts  1.58 us

profile of v7, /device:TPU:0, one launch (start us, length us, event | category | flops | bytes accessed | tf_op | source)
XLA Modules:
  0.0 66.1 jit_solution(10923286715391563098)
XLA Ops:
  0.0 0.0 copy-start.3
  0.0 0.8 %copy_bitcast_fusion = (bf16[1,16,4,128]{3,1,0,2:T(8,128)(2,1)S(1)}, bf16[1,16,4,128]{3,1,0,2:T(8,128)(2,1)S(1)}) fusion(bf16[16,4,128]{2,1,0:T(4,128)(2,1)} %param.9, bf16[16,4,128]{2,1,0:T(4,128)(2,1)} %param.8), kind=kLoop, calls=%fused_computation.2 | loop fusion | bytes 65536 | tf_op jit(solution)/shard_map/stack | solution.py:439
  0.8 1.1 %copy.8 = bf16[4,3,128,128]{3,2,1,0:T(8,128)(2,1)S(1)} copy(bf16[4,3,128,128]{3,0,2,1:T(4,128)(2,1)} %bitcast.16) | data formatting | bytes 786432 | tf_op jit(solution)/shard_map/transpose | solution.py:437
  1.9 0.0 copy-done.3
  1.9 0.3 copy.9
  2.2 0.0 copy-start
  2.2 0.0 copy-start.1
  2.2 0.0 copy-start.2
  2.2 0.1 pad_maximum_fusion.refs_1_
  2.3 0.9 %copy-done = bf16[8,128,128]{2,1,0:T(8,128)(2,1)S(1)} copy-done((bf16[8,128,128]{2,1,0:T(8,128)(2,1)S(1)}, bf16[8,128,128]{2,1,0:T(8,128)(2,1)}, u32[]{:S(2)}) %copy-start) | copy-done | bytes 262168
  3.1 0.0 copy-done.1
  3.1 0.0 copy-done.2
  3.1 62.3 %shard_map.73 = bf16[8,128,128]{2,1,0:T(8,128)(2,1)S(1)} custom-call(bf16[8,128,128]{2,1,0:T(8,128)(2,1)S(1)} %copy-done, bf16[4,2,400,128]{3,2,1,0:T(8,128)(2,1)S(1)} %pad_maximum_fusion.refs_1_, s32[1,16]{1,0:T(1,128)S(1)} %bitcast.12, s32[1,32]{1,0:T(1,128)S(1)} %bitcast.13), custom_call_target="tpu_custom_call" | custom-call | flops 3355443200 | bytes 1343488 | tf_op jit(solution)/shard_map/pallas_call | solution.py:465
  65.4 0.7 %copy.15 = bf16[8,128,128]{2,1,0:T(8,128)(2,1)} copy(bf16[8,128,128]{2,1,0:T(8,128)(2,1)S(1)} %shard_map.73) | data formatting | bytes 524288
  (1 shorter events, 0.0 us)
Async XLA Ops:
  0.0 1.9 %copy-start.3 = (bf16[3,128,4,128]{3,2,1,0:T(4,128)(2,1)S(1)}, bf16[3,128,4,128]{3,2,1,0:T(4,128)(2,1)}, u32[]{:S(2)}) copy-start(bf16[3,128,4,128]{3,2,1,0:T(4,128)(2,1)} %param.12) | copy-start | bytes 1179652
  2.2 1.0 %copy-start = (bf16[8,128,128]{2,1,0:T(8,128)(2,1)S(1)}, bf16[8,128,128]{2,1,0:T(8,128)(2,1)}, u32[]{:S(2)}) copy-start(bf16[8,128,128]{2,1,0:T(8,128)(2,1)} %refs_0_.1) | copy-start | bytes 786436
  2.2 0.9 %copy-start.1 = (s32[16]{0:T(128)S(1)}, s32[16]{0:T(128)}, u32[]{:S(2)}) copy-start(s32[16]{0:T(128)} %param.10) | copy-start | bytes 196
  2.2 0.9 %copy-start.2 = (s32[32]{0:T(128)S(1)}, s32[32]{0:T(128)}, u32[]{:S(2)}) copy-start(s32[32]{0:T(128)} %param.13) | copy-start | bytes 388

commit v8 on v7

--- a/solution.py
+++ b/solution.py
@@ -9,8 +9,8 @@
 
 MESH = pl.DeviceIdType.MESH
 NEG = -1e30
-FIRST_DELAY = 3
-HOP_DELAY = 1
+FIRST_DELAY = 5
+HOP_DELAY = 3
 
 
 def split_ctx(n):

time: 66.3 us -> 58.9 us (0.89)
  Pallas kernels: 62.3 us -> 54.8 us
    pallas_call x1, Pallas kernels: 62.3 us -> 54.8 us  [body(): pl.pallas_call(lambda *refs: kernel(dims, *refs), out_shape=jax.ShapeDtyp...]
where the time goes in v8:
time: 58.9 us; the launch traced here: 58.7 us
  Pallas kernels  54.8 us (93%)
  local copies, waits for them, and re-layouts  3.73 us (6%)
    pallas_call x1, Pallas kernels, body(): pl.pallas_call(lambda *refs: kernel(dims, *refs), out_shape=jax.ShapeDtyp...  54.8 us
    unnamed x9, local copies, waits for them, and re-layouts  1.58 us

profile of v8, /device:TPU:0, one launch (start us, length us, event | category | flops | bytes accessed | tf_op | source)
XLA Modules:
  0.0 58.7 jit_solution(16531457916511922392)
XLA Ops:
  0.0 0.0 copy-start.3
  0.0 0.8 %copy_bitcast_fusion = (bf16[1,16,4,128]{3,1,0,2:T(8,128)(2,1)S(1)}, bf16[1,16,4,128]{3,1,0,2:T(8,128)(2,1)S(1)}) fusion(bf16[16,4,128]{2,1,0:T(4,128)(2,1)} %param.9, bf16[16,4,128]{2,1,0:T(4,128)(2,1)} %param.8), kind=kLoop, calls=%fused_computation.2 | loop fusion | bytes 65536 | tf_op jit(solution)/shard_map/stack | solution.py:439
  0.8 1.1 %copy.8 = bf16[4,3,128,128]{3,2,1,0:T(8,128)(2,1)S(1)} copy(bf16[4,3,128,128]{3,0,2,1:T(4,128)(2,1)} %bitcast.16) | data formatting | bytes 786432 | tf_op jit(solution)/shard_map/transpose | solution.py:437
  1.9 0.0 copy-done.3
  1.9 0.3 copy.9
  2.2 0.0 copy-start
  2.2 0.0 copy-start.1
  2.2 0.0 copy-start.2
  2.2 0.1 pad_maximum_fusion.refs_1_
  2.3 0.9 %copy-done = bf16[8,128,128]{2,1,0:T(8,128)(2,1)S(1)} copy-done((bf16[8,128,128]{2,1,0:T(8,128)(2,1)S(1)}, bf16[8,128,128]{2,1,0:T(8,128)(2,1)}, u32[]{:S(2)}) %copy-start) | copy-done | bytes 262168
  3.1 0.0 copy-done.1
  3.1 0.0 copy-done.2
  3.1 54.8 %shard_map.73 = bf16[8,128,128]{2,1,0:T(8,128)(2,1)S(1)} custom-call(bf16[8,128,128]{2,1,0:T(8,128)(2,1)S(1)} %copy-done, bf16[4,2,400,128]{3,2,1,0:T(8,128)(2,1)S(1)} %pad_maximum_fusion.refs_1_, s32[1,16]{1,0:T(1,128)S(1)} %bitcast.12, s32[1,32]{1,0:T(1,128)S(1)} %bitcast.13), custom_call_target="tpu_custom_call" | custom-call | flops 3355443200 | bytes 1343488 | tf_op jit(solution)/shard_map/pallas_call | solution.py:465
  58.0 0.7 %copy.15 = bf16[8,128,128]{2,1,0:T(8,128)(2,1)} copy(bf16[8,128,128]{2,1,0:T(8,128)(2,1)S(1)} %shard_map.73) | data formatting | bytes 524288
  (1 shorter events, 0.0 us)
Async XLA Ops:
  0.0 1.9 %copy-start.3 = (bf16[3,128,4,128]{3,2,1,0:T(4,128)(2,1)S(1)}, bf16[3,128,4,128]{3,2,1,0:T(4,128)(2,1)}, u32[]{:S(2)}) copy-start(bf16[3,128,4,128]{3,2,1,0:T(4,128)(2,1)} %param.12) | copy-start | bytes 1179652
  2.2 1.0 %copy-start = (bf16[8,128,128]{2,1,0:T(8,128)(2,1)S(1)}, bf16[8,128,128]{2,1,0:T(8,128)(2,1)}, u32[]{:S(2)}) copy-start(bf16[8,128,128]{2,1,0:T(8,128)(2,1)} %refs_0_.1) | copy-start | bytes 786436
  2.2 0.9 %copy-start.1 = (s32[16]{0:T(128)S(1)}, s32[16]{0:T(128)}, u32[]{:S(2)}) copy-start(s32[16]{0:T(128)} %param.10) | copy-start | bytes 196
  2.2 0.9 %copy-start.2 = (s32[32]{0:T(128)S(1)}, s32[32]{0:T(128)}, u32[]{:S(2)}) copy-start(s32[32]{0:T(128)} %param.13) | copy-start | bytes 388

commit v9 on v8

--- a/solution.py
+++ b/solution.py
@@ -9,8 +9,8 @@
 
 MESH = pl.DeviceIdType.MESH
 NEG = -1e30
-FIRST_DELAY = 5
-HOP_DELAY = 3
+FIRST_DELAY = 7
+HOP_DELAY = 4
 
 
 def split_ctx(n):

time: 58.9 us -> 59.3 us (level)
  no operation moved by 1% of the time
where the time goes in v9:
time: 59.3 us; the launch traced here: 59.1 us
  Pallas kernels  55.2 us (93%)
  local copies, waits for them, and re-layouts  3.73 us (6%)
    pallas_call x1, Pallas kernels, body(): pl.pallas_call(lambda *refs: kernel(dims, *refs), out_shape=jax.ShapeDtyp...  55.2 us
    unnamed x9, local copies, waits for them, and re-layouts  1.58 us

profile of v9, /device:TPU:0, one launch (start us, length us, event | category | flops | bytes accessed | tf_op | source)
XLA Modules:
  0.0 59.1 jit_solution(12164320868170935175)
XLA Ops:
  0.0 0.0 copy-start.3
  0.0 0.8 %copy_bitcast_fusion = (bf16[1,16,4,128]{3,1,0,2:T(8,128)(2,1)S(1)}, bf16[1,16,4,128]{3,1,0,2:T(8,128)(2,1)S(1)}) fusion(bf16[16,4,128]{2,1,0:T(4,128)(2,1)} %param.9, bf16[16,4,128]{2,1,0:T(4,128)(2,1)} %param.8), kind=kLoop, calls=%fused_computation.2 | loop fusion | bytes 65536 | tf_op jit(solution)/shard_map/stack | solution.py:439
  0.8 1.1 %copy.8 = bf16[4,3,128,128]{3,2,1,0:T(8,128)(2,1)S(1)} copy(bf16[4,3,128,128]{3,0,2,1:T(4,128)(2,1)} %bitcast.16) | data formatting | bytes 786432 | tf_op jit(solution)/shard_map/transpose | solution.py:437
  1.9 0.0 copy-done.3
  1.9 0.3 copy.9
  2.2 0.0 copy-start
  2.2 0.0 copy-start.1
  2.2 0.0 copy-start.2
  2.2 0.1 pad_maximum_fusion.refs_1_
  2.3 0.9 %copy-done = bf16[8,128,128]{2,1,0:T(8,128)(2,1)S(1)} copy-done((bf16[8,128,128]{2,1,0:T(8,128)(2,1)S(1)}, bf16[8,128,128]{2,1,0:T(8,128)(2,1)}, u32[]{:S(2)}) %copy-start) | copy-done | bytes 262168
  3.1 0.0 copy-done.1
  3.1 0.0 copy-done.2
  3.1 55.2 %shard_map.73 = bf16[8,128,128]{2,1,0:T(8,128)(2,1)S(1)} custom-call(bf16[8,128,128]{2,1,0:T(8,128)(2,1)S(1)} %copy-done, bf16[4,2,400,128]{3,2,1,0:T(8,128)(2,1)S(1)} %pad_maximum_fusion.refs_1_, s32[1,16]{1,0:T(1,128)S(1)} %bitcast.12, s32[1,32]{1,0:T(1,128)S(1)} %bitcast.13), custom_call_target="tpu_custom_call" | custom-call | flops 3355443200 | bytes 1343488 | tf_op jit(solution)/shard_map/pallas_call | solution.py:465
  58.3 0.7 %copy.15 = bf16[8,128,128]{2,1,0:T(8,128)(2,1)} copy(bf16[8,128,128]{2,1,0:T(8,128)(2,1)S(1)} %shard_map.73) | data formatting | bytes 524288
  (1 shorter events, 0.0 us)
Async XLA Ops:
  0.0 1.9 %copy-start.3 = (bf16[3,128,4,128]{3,2,1,0:T(4,128)(2,1)S(1)}, bf16[3,128,4,128]{3,2,1,0:T(4,128)(2,1)}, u32[]{:S(2)}) copy-start(bf16[3,128,4,128]{3,2,1,0:T(4,128)(2,1)} %param.12) | copy-start | bytes 1179652
  2.2 1.0 %copy-start = (bf16[8,128,128]{2,1,0:T(8,128)(2,1)S(1)}, bf16[8,128,128]{2,1,0:T(8,128)(2,1)}, u32[]{:S(2)}) copy-start(bf16[8,128,128]{2,1,0:T(8,128)(2,1)} %refs_0_.1) | copy-start | bytes 786436
  2.2 0.9 %copy-start.1 = (s32[16]{0:T(128)S(1)}, s32[16]{0:T(128)}, u32[]{:S(2)}) copy-start(s32[16]{0:T(128)} %param.10) | copy-start | bytes 196
  2.2 0.9 %copy-start.2 = (s32[32]{0:T(128)S(1)}, s32[32]{0:T(128)}, u32[]{:S(2)}) copy-start(s32[32]{0:T(128)} %param.13) | copy-start | bytes 388

commit v10 on v8

--- a/solution.py
+++ b/solution.py
@@ -311,7 +311,7 @@
                 def _():
                     q_forward(h + 1, d)
 
-            @pl.when((h + 1 < H) & (j == max(A - 2, 0)))
+            @pl.when((h + 1 < H) & (j == A - 1))
             def _():
                 kv_stage1(h + 1)
 

time: 58.9 us -> 61 us (1.036)
  Pallas kernels: 54.8 us -> 57 us
    pallas_call x1, Pallas kernels: 54.8 us -> 57 us  [body(): pl.pallas_call(lambda *refs: kernel(dims, *refs), out_shape=jax.ShapeDtyp...]
where the time goes in v10:
time: 61 us; the launch traced here: 60.8 us
  Pallas kernels  57 us (93%)
  local copies, waits for them, and re-layouts  3.73 us (6%)
    pallas_call x1, Pallas kernels, body(): pl.pallas_call(lambda *refs: kernel(dims, *refs), out_shape=jax.ShapeDtyp...  57 us
    unnamed x9, local copies, waits for them, and re-layouts  1.58 us

profile of v10, /device:TPU:0, one launch (start us, length us, event | category | flops | bytes accessed | tf_op | source)
XLA Modules:
  0.0 60.8 jit_solution(13526034505296086974)
XLA Ops:
  0.0 0.0 copy-start.3
  0.0 0.8 %copy_bitcast_fusion = (bf16[1,16,4,128]{3,1,0,2:T(8,128)(2,1)S(1)}, bf16[1,16,4,128]{3,1,0,2:T(8,128)(2,1)S(1)}) fusion(bf16[16,4,128]{2,1,0:T(4,128)(2,1)} %param.9, bf16[16,4,128]{2,1,0:T(4,128)(2,1)} %param.8), kind=kLoop, calls=%fused_computation.2 | loop fusion | bytes 65536 | tf_op jit(solution)/shard_map/stack | solution.py:439
  0.8 1.1 %copy.8 = bf16[4,3,128,128]{3,2,1,0:T(8,128)(2,1)S(1)} copy(bf16[4,3,128,128]{3,0,2,1:T(4,128)(2,1)} %bitcast.16) | data formatting | bytes 786432 | tf_op jit(solution)/shard_map/transpose | solution.py:437
  1.9 0.0 copy-done.3
  1.9 0.3 copy.9
  2.2 0.0 copy-start
  2.2 0.0 copy-start.1
  2.2 0.0 copy-start.2
  2.2 0.1 pad_maximum_fusion.refs_1_
  2.3 0.9 %copy-done = bf16[8,128,128]{2,1,0:T(8,128)(2,1)S(1)} copy-done((bf16[8,128,128]{2,1,0:T(8,128)(2,1)S(1)}, bf16[8,128,128]{2,1,0:T(8,128)(2,1)}, u32[]{:S(2)}) %copy-start) | copy-done | bytes 262168
  3.1 0.0 copy-done.1
  3.1 0.0 copy-done.2
  3.1 57.0 %shard_map.73 = bf16[8,128,128]{2,1,0:T(8,128)(2,1)S(1)} custom-call(bf16[8,128,128]{2,1,0:T(8,128)(2,1)S(1)} %copy-done, bf16[4,2,400,128]{3,2,1,0:T(8,128)(2,1)S(1)} %pad_maximum_fusion.refs_1_, s32[1,16]{1,0:T(1,128)S(1)} %bitcast.12, s32[1,32]{1,0:T(1,128)S(1)} %bitcast.13), custom_call_target="tpu_custom_call" | custom-call | flops 3355443200 | bytes 1343488 | tf_op jit(solution)/shard_map/pallas_call | solution.py:465
  60.1 0.7 %copy.15 = bf16[8,128,128]{2,1,0:T(8,128)(2,1)} copy(bf16[8,128,128]{2,1,0:T(8,128)(2,1)S(1)} %shard_map.73) | data formatting | bytes 524288
  (1 shorter events, 0.0 us)
Async XLA Ops:
  0.0 1.9 %copy-start.3 = (bf16[3,128,4,128]{3,2,1,0:T(4,128)(2,1)S(1)}, bf16[3,128,4,128]{3,2,1,0:T(4,128)(2,1)}, u32[]{:S(2)}) copy-start(bf16[3,128,4,128]{3,2,1,0:T(4,128)(2,1)} %param.12) | copy-start | bytes 1179652
  2.2 1.0 %copy-start = (bf16[8,128,128]{2,1,0:T(8,128)(2,1)S(1)}, bf16[8,128,128]{2,1,0:T(8,128)(2,1)}, u32[]{:S(2)}) copy-start(bf16[8,128,128]{2,1,0:T(8,128)(2,1)} %refs_0_.1) | copy-start | bytes 786436
  2.2 0.9 %copy-start.1 = (s32[16]{0:T(128)S(1)}, s32[16]{0:T(128)}, u32[]{:S(2)}) copy-start(s32[16]{0:T(128)} %param.10) | copy-start | bytes 196
  2.2 0.9 %copy-start.2 = (s32[32]{0:T(128)S(1)}, s32[32]{0:T(128)}, u32[]{:S(2)}) copy-start(s32[32]{0:T(128)} %param.13) | copy-start | bytes 388

commit v11 on v10

--- a/solution.py
+++ b/solution.py
@@ -311,7 +311,7 @@
                 def _():
                     q_forward(h + 1, d)
 
-            @pl.when((h + 1 < H) & (j == A - 1))
+            @pl.when((h + 1 < H) & (j == 0))
             def _():
                 kv_stage1(h + 1)
 

time: 61 us -> 61.1 us (level)
  no operation moved by 1% of the time
where the time goes in v11:
time: 61.1 us; the launch traced here: 60.8 us
  Pallas kernels  57 us (93%)
  local copies, waits for them, and re-layouts  3.73 us (6%)
    pallas_call x1, Pallas kernels, body(): pl.pallas_call(lambda *refs: kernel(dims, *refs), out_shape=jax.ShapeDtyp...  57 us
    unnamed x9, local copies, waits for them, and re-layouts  1.58 us

profile of v11, /device:TPU:0, one launch (start us, length us, event | category | flops | bytes accessed | tf_op | source)
XLA Modules:
  0.0 60.8 jit_solution(4755887088047331354)
XLA Ops:
  0.0 0.0 copy-start.3
  0.0 0.8 %copy_bitcast_fusion = (bf16[1,16,4,128]{3,1,0,2:T(8,128)(2,1)S(1)}, bf16[1,16,4,128]{3,1,0,2:T(8,128)(2,1)S(1)}) fusion(bf16[16,4,128]{2,1,0:T(4,128)(2,1)} %param.9, bf16[16,4,128]{2,1,0:T(4,128)(2,1)} %param.8), kind=kLoop, calls=%fused_computation.2 | loop fusion | bytes 65536 | tf_op jit(solution)/shard_map/stack | solution.py:439
  0.8 1.1 %copy.8 = bf16[4,3,128,128]{3,2,1,0:T(8,128)(2,1)S(1)} copy(bf16[4,3,128,128]{3,0,2,1:T(4,128)(2,1)} %bitcast.16) | data formatting | bytes 786432 | tf_op jit(solution)/shard_map/transpose | solution.py:437
  1.9 0.0 copy-done.3
  1.9 0.3 copy.9
  2.2 0.0 copy-start
  2.2 0.0 copy-start.1
  2.2 0.0 copy-start.2
  2.2 0.1 pad_maximum_fusion.refs_1_
  2.3 0.9 %copy-done = bf16[8,128,128]{2,1,0:T(8,128)(2,1)S(1)} copy-done((bf16[8,128,128]{2,1,0:T(8,128)(2,1)S(1)}, bf16[8,128,128]{2,1,0:T(8,128)(2,1)}, u32[]{:S(2)}) %copy-start) | copy-done | bytes 262168
  3.1 0.0 copy-done.1
  3.1 0.0 copy-done.2
  3.1 57.0 %shard_map.73 = bf16[8,128,128]{2,1,0:T(8,128)(2,1)S(1)} custom-call(bf16[8,128,128]{2,1,0:T(8,128)(2,1)S(1)} %copy-done, bf16[4,2,400,128]{3,2,1,0:T(8,128)(2,1)S(1)} %pad_maximum_fusion.refs_1_, s32[1,16]{1,0:T(1,128)S(1)} %bitcast.12, s32[1,32]{1,0:T(1,128)S(1)} %bitcast.13), custom_call_target="tpu_custom_call" | custom-call | flops 3355443200 | bytes 1343488 | tf_op jit(solution)/shard_map/pallas_call | solution.py:465
  60.1 0.7 %copy.15 = bf16[8,128,128]{2,1,0:T(8,128)(2,1)} copy(bf16[8,128,128]{2,1,0:T(8,128)(2,1)S(1)} %shard_map.73) | data formatting | bytes 524288
  (1 shorter events, 0.0 us)
Async XLA Ops:
  0.0 1.9 %copy-start.3 = (bf16[3,128,4,128]{3,2,1,0:T(4,128)(2,1)S(1)}, bf16[3,128,4,128]{3,2,1,0:T(4,128)(2,1)}, u32[]{:S(2)}) copy-start(bf16[3,128,4,128]{3,2,1,0:T(4,128)(2,1)} %param.12) | copy-start | bytes 1179652
  2.2 1.0 %copy-start = (bf16[8,128,128]{2,1,0:T(8,128)(2,1)S(1)}, bf16[8,128,128]{2,1,0:T(8,128)(2,1)}, u32[]{:S(2)}) copy-start(bf16[8,128,128]{2,1,0:T(8,128)(2,1)} %refs_0_.1) | copy-start | bytes 786436
  2.2 0.9 %copy-start.1 = (s32[16]{0:T(128)S(1)}, s32[16]{0:T(128)}, u32[]{:S(2)}) copy-start(s32[16]{0:T(128)} %param.10) | copy-start | bytes 196
  2.2 0.9 %copy-start.2 = (s32[32]{0:T(128)S(1)}, s32[32]{0:T(128)}, u32[]{:S(2)}) copy-start(s32[32]{0:T(128)} %param.13) | copy-start | bytes 388
